TPU v7x, 128 devices: a whole 4x4x4 slice. The times are simulated.
128 devices in a mesh: pair: 8 (over x, z_hi), ctr: 16 (over y, z_lo, core).
Axes of the slice: x: 4, y: 4, z: 4 (z_hi: 2, z_lo: 2; z = z_hi * 2 + z_lo), core: 2. Of those that a mesh axis runs over, the one named last changes fastest.
Arguments:
- amplitudes: bfloat16 [4096, 32768], P('pair', 'ctr'), may hold values from -6 to 6
- v_plus: bfloat16 [32768, 2048], P('ctr'), may hold values from -0.046875 to 0.046875
- v_minus: bfloat16 [32768, 2048], P('ctr'), may hold values from -0.046875 to 0.046875
- occ_irrep: int32 [64], replicated, may hold values from 0 to 7
- col_irrep: int32 [32768], P('ctr'), may hold values from 0 to 7
- block_map: int32 [8, 8], replicated, may hold values 0 or 1
Outputs:
- residual: bfloat16 [2048, 4096], P('ctr', 'pair')
All inputs are finite; a program needn't handle non-finite values.
Results may differ from a plain program's by a relative error of at most 0.0052.
Values may be sent and summed in bfloat16 or wider, within the bound.
No kernel may reach another device: no remote copies, remote signals or barrier semaphores. Data moves between devices by JAX's collectives and lax.ppermute only.
A program may use at most 128 MiB of HBM per device.

v0:
```python
import jax
import jax.numpy as jnp
from jax import lax
from jax.sharding import PartitionSpec as P


def body(amplitudes, v_plus, v_minus, occ_irrep, col_irrep, block_map):
    groups = lax.axis_size("pair")
    rows, depth = amplitudes.shape
    orbitals = occ_irrep.shape[0]
    own = orbitals // groups
    blocks = amplitudes.reshape(own, groups, own, depth)
    arrived = lax.all_to_all(blocks, "pair", split_axis=1, concat_axis=1, tiled=True)
    partner = jnp.transpose(arrived, (2, 1, 0, 3)).reshape(rows, depth)
    my_irreps = lax.dynamic_slice_in_dim(occ_irrep, lax.axis_index("pair") * own, own)
    pair_irrep = jnp.bitwise_xor(my_irreps[:, None], occ_irrep[None, :]).reshape(rows)
    labels = jnp.arange(block_map.shape[0], dtype=jnp.int32)
    row_onehot = (pair_irrep[:, None] == labels[None, :]).astype(jnp.float32)
    row_table = jnp.dot(row_onehot, block_map.astype(jnp.float32))
    col_onehot = (labels[:, None] == col_irrep[None, :]).astype(jnp.float32)
    keep = jnp.dot(row_table, col_onehot)
    own_f = amplitudes.astype(jnp.float32)
    par_f = partner.astype(jnp.float32)
    sym = (keep * (own_f + par_f)).astype(jnp.bfloat16)
    anti = (keep * (own_f - par_f)).astype(jnp.bfloat16)
    width = v_plus.shape[1]
    slabs = lax.axis_size("ctr")
    share = width // slabs
    dims = (((0,), (1,)), ((), ()))
    first = lax.dot_general(v_plus, sym, dims, preferred_element_type=jnp.float32)
    second = lax.dot_general(v_minus, anti, dims, preferred_element_type=jnp.float32)
    summed = lax.psum(0.5 * (first + second), "ctr")
    mine = lax.dynamic_slice_in_dim(summed, lax.axis_index("ctr") * share, share, 0)
    return mine.astype(jnp.bfloat16)


def solution(mesh):
    in_specs = (P("pair", "ctr"), P("ctr", None), P("ctr", None), P(), P("ctr"), P())
    out_specs = P("ctr", "pair")
    return jax.shard_map(body, mesh=mesh, in_specs=in_specs, out_specs=out_specs, check_vma=False)
```

profile of v0, /device:TPU:1, one launch (start us, length us, event | category | flops | bytes accessed | tf_op | source)
XLA Modules:
  0.0 167.3 jit_solution(8198435474187161643)
XLA Ops:
  0.0 0.0 copy-start.4
  0.0 4.3 %copy.11 = bf16[8,8,8,2048]{3,0,2,1:T(8,128)(2,1)} copy(bf16[8,8,8,2048]{3,2,1,0:T(8,128)(2,1)} %bitcast.12) | data formatting | bytes 4194304 | tf_op jit(solution)/shard_map/reshape | solution.py:12
  4.3 8.2 %all-to-all-start = ((bf16[8,8,8,2048]{3,0,2,1:T(8,128)(2,1)}), bf16[8,8,8,2048]{3,0,2,1:T(8,128)(2,1)S(1)}, u32[]{:S(2)}, u32[]{:S(2)}) async-start(bf16[8,8,8,2048]{3,0,2,1:T(8,128)(2,1)} %copy.11), calls=%async_computation | async-start | bytes 4194304 | tf_op jit(solution)/shard_map/all_to_all | solution.py:13
  12.4 0.0 copy-done.4
  12.4 0.1 dynamic_slice.6
  12.5 0.1 broadcast_xor_fusion
  12.6 0.1 xor.23
  12.7 30.3 %all-to-all-done = bf16[8,8,8,2048]{3,0,2,1:T(8,128)(2,1)S(1)} async-done(((bf16[8,8,8,2048]{3,0,2,1:T(8,128)(2,1)}), bf16[8,8,8,2048]{3,0,2,1:T(8,128)(2,1)S(1)}, u32[]{:S(2)}, u32[]{:S(2)}) %all-to-all-start) | async-done | bytes 2097184 | tf_op jit(solution)/shard_map/all_to_all | solution.py:13
  42.9 0.5 convert_bitcast_fusion
  43.4 0.0 copy-start
  43.5 0.0 copy-start.2
  43.5 0.0 copy-start.3
  43.5 2.2 %copy.12 = f32[8,8,8,2048]{3,2,1,0:T(8,128)} copy(f32[8,8,8,2048]{3,2,0,1:T(8,128)S(1)} %convert_bitcast_fusion) | data formatting | bytes 8388608 | tf_op jit(solution)/shard_map/convert_element_type | solution.py:23
  45.7 0.1 copy-done
  45.8 0.0 copy-done.2
  45.8 0.0 copy-done.3
  45.8 5.4 %fusion.3 = (bf16[512,2048]{1,0:T(8,128)(2,1)}, bf16[512,2048]{1,0:T(8,128)(2,1)}) fusion(bf16[512,2048]{1,0:T(8,128)(2,1)S(1)} %copy-done, f32[8,8,8,2048]{3,2,1,0:T(8,128)} %copy.12, s32[2048]{0:T(1024)S(1)} %copy-done.2, s32[512]{0:T(512)S(1)} %xor.23, s32[8,8]{1,0:T(8,128)S(1)} %copy-done.3), kind=kOutput, calls=%fused_computation.5 | convolution fusion | flops 24203328 | bytes 10496256 | tf_op jit(solution)/shard_map/dot_general | solution.py:21
  51.2 0.0 copy-start.1
  51.2 7.7 %fusion.14 = f32[512,2048]{1,0:T(8,128)S(1)} fusion(bf16[512,2048]{1,0:T(8,128)(2,1)} %get-tuple-element.6, bf16[2048,2048]{1,0:T(8,128)(2,1)} %param.7), kind=kOutput, calls=%fused_computation.17 | convolution fusion | flops 4294967296 | bytes 14680064 | tf_op jit(solution)/shard_map/dot_general | solution.py:30
  58.9 0.0 copy-done.1
  59.0 9.6 %multiply_bitcast_fusion = f32[2048,512]{0,1:T(8,128)} fusion(f32[512,2048]{1,0:T(8,128)S(1)} %fusion.14, bf16[512,2048]{1,0:T(8,128)(2,1)S(1)} %copy-done.1, bf16[2048,2048]{1,0:T(8,128)(2,1)} %param.8), kind=kOutput, calls=%fused_computation.7 | convolution fusion | flops 4297064448 | bytes 18874368 | tf_op jit(solution)/shard_map/dot_general | solution.py:31
  68.6 97.9 %all-reduce.1 = bf16[2048,512]{0,1:T(8,128)(2,1)S(1)} all-reduce(f32[2048,512]{0,1:T(8,128)} %multiply_bitcast_fusion), channel_id=1, replica_groups=mesh['pair'=8,'ctr'=16] {'ctr'}, use_global_device_ids=true, to_apply=%region_0.0 | all-reduce | flops 1048576 | bytes 6291456 | tf_op jit(solution)/shard_map/psum | solution.py:32
  166.5 0.8 copy.13
  (1 shorter events, 0.0 us)
Async XLA Ops:
  0.0 12.4 %copy-start.4 = (s32[64]{0:T(128)S(1)}, s32[64]{0:T(128)}, u32[]{:S(2)}) copy-start(s32[64]{0:T(128)} %param.9) | copy-start | bytes 772
  4.3 38.7 %all-to-all-start = ((bf16[8,8,8,2048]{3,0,2,1:T(8,128)(2,1)}), bf16[8,8,8,2048]{3,0,2,1:T(8,128)(2,1)S(1)}, u32[]{:S(2)}, u32[]{:S(2)}) async-start(bf16[8,8,8,2048]{3,0,2,1:T(8,128)(2,1)} %copy.11), calls=%async_computation | async-start | bytes 4194304 | tf_op jit(solution)/shard_map/all_to_all | solution.py:13
  43.4 2.4 %copy-start = (bf16[512,2048]{1,0:T(8,128)(2,1)S(1)}, bf16[512,2048]{1,0:T(8,128)(2,1)}, u32[]{:S(2)}) copy-start(bf16[512,2048]{1,0:T(8,128)(2,1)} %param.6) | copy-start | bytes 6291460
  43.5 2.4 %copy-start.2 = (s32[2048]{0:T(1024)S(1)}, s32[2048]{0:T(1024)}, u32[]{:S(2)}) copy-start(s32[2048]{0:T(1024)} %param.10) | copy-start | bytes 24580
  43.5 2.4 %copy-start.3 = (s32[8,8]{1,0:T(8,128)S(1)}, s32[8,8]{1,0:T(8,128)}, u32[]{:S(2)}) copy-start(s32[8,8]{1,0:T(8,128)} %param.11) | copy-start | bytes 772
  51.2 7.7 %copy-start.1 = (bf16[512,2048]{1,0:T(8,128)(2,1)S(1)}, bf16[512,2048]{1,0:T(8,128)(2,1)}, u32[]{:S(2)}) copy-start(bf16[512,2048]{1,0:T(8,128)(2,1)} %get-tuple-element.5) | copy-start | bytes 6291460
where the time goes:
time: 168 us; the launch traced here: 167 us
  blocking collectives  97.9 us (58%)
  waiting for transfers between devices  30.3 us (18%)
  matrix products  22.7 us (14%)
  starting transfers between devices  8.16 us (5%)
  local copies, waits for them, and re-layouts  7.59 us (5%)
    psum x1, blocking collectives, body(): summed = lax.psum(0.5 * (first + second), 'ctr')  97.9 us
    all_to_all x1, waiting for transfers between devices, body(): lax.all_to_all(blocks, 'pair', split_axis=1, concat_axis=1, tiled=True)  30.3 us
    dot_general x1, matrix products, body(): lax.dot_general(v_minus, anti, dims, preferred_element_type=jnp.float32)  9.61 us
    all_to_all x1, starting transfers between devices, body(): lax.all_to_all(blocks, 'pair', split_axis=1, concat_axis=1, tiled=True)  8.16 us
    dot_general x1, matrix products, body(): lax.dot_general(v_plus, sym, dims, preferred_element_type=jnp.float32)  7.7 us
    dot_general x1, matrix products, body(): keep = jnp.dot(row_table, col_onehot)  5.41 us
    reshape x1, local copies, waits for them, and re-layouts, body(): blocks = amplitudes.reshape(own, groups, own, depth)  4.26 us
  transfers between devices with their start and end apart: 1, of which 1 were waited for; matrix products, arithmetic and copies ran while one was open for 0% of the time, Pallas kernels for 0%

commit v1 on v0

v1 whole, which is shorter than its diff:
```python
import functools

import jax
import jax.numpy as jnp
from jax import lax
from jax.experimental import pallas as pl
from jax.experimental.pallas import tpu as pltpu
from jax.sharding import Mesh, PartitionSpec as P

F32, BF16 = jnp.float32, jnp.bfloat16
LANES = 128
MIB = 1 << 20


def mask_rows(where_ref, occ_ref, map_ref, occ_col_ref, col_ref, t_ref, tm_ref):
    orbitals = occ_col_ref.shape[0]
    own = t_ref.shape[0] // orbitals
    irreps = map_ref.shape[0]
    kept = []
    for r in range(irreps):
        word = map_ref[r, 0]
        for c in range(1, irreps):
            word = word + map_ref[r, c] * (1 << c)
        kept.append(word)
    col = col_ref[...]
    for a in range(own):
        pair = occ_col_ref[...] ^ occ_ref[where_ref[0] * own + a]
        word = jnp.zeros_like(pair)
        for r in range(irreps):
            word = jnp.where(pair == r, kept[r], word)
        keep = jnp.right_shift(word, col) & 1
        rows = pl.ds(a * orbitals, orbitals)
        tm_ref[rows, :] = jnp.where(keep == 1, t_ref[rows, :].astype(F32), 0.0).astype(BF16)


def split_cores(core, acc, shape, keep_ref, send_ref, swap):
    low, high = acc[:, :LANES], acc[:, LANES:]
    mine = jnp.where(core == 0, low, high)
    other = jnp.where(core == 0, high, low)
    if swap:
        mine = jnp.swapaxes(mine.reshape(shape), 0, 1)
        other = jnp.swapaxes(other.reshape(shape), 0, 1)
    keep_ref[0] = mine.reshape(acc.shape[0], LANES)
    send_ref[0] = other.reshape(acc.shape[0], LANES).astype(BF16)


def v_kernel(where_ref, occ_ref, map_ref, occ_col_ref, col_ref, t_ref, p_ref, m_ref, keep_ref, send_ref, tm_ref):
    @pl.when(pl.program_id(0) == 0)
    def _():
        mask_rows(where_ref, occ_ref, map_ref, occ_col_ref, col_ref, t_ref, tm_ref)

    w = (p_ref[...].astype(F32) - m_ref[...].astype(F32)).astype(BF16)
    acc = jnp.dot(tm_ref[...], w, preferred_element_type=F32)
    own = t_ref.shape[0] // occ_col_ref.shape[0]
    shape = (own, occ_col_ref.shape[0] // own, own, LANES)
    split_cores(where_ref[1], acc, shape, keep_ref, send_ref, True)


def u_kernel(where_ref, tm_ref, p_ref, m_ref, keep_ref, send_ref):
    w = (p_ref[...].astype(F32) + m_ref[...].astype(F32)).astype(BF16)
    acc = jnp.dot(tm_ref[...], w, preferred_element_type=F32)
    split_cores(where_ref[1], acc, None, keep_ref, send_ref, False)


def last_kernel(own, u_ref, v_ref, out_ref, scratch):
    slabs, rows, _ = u_ref.shape
    u = u_ref[0].astype(F32)
    v = v_ref[0].astype(F32)
    for s in range(1, slabs):
        u = u + u_ref[s].astype(F32)
        v = v + v_ref[s].astype(F32)
    scratch[...] = v
    orbitals = rows // own
    parts = [scratch[pl.ds(b, orbitals, stride=own), :] for b in range(own)]
    total = 0.5 * (u + jnp.concatenate(parts, axis=0))
    out_ref[...] = total.T.astype(BF16)


def whole(shape):
    return pl.BlockSpec(shape, lambda s, *_: (0,) * len(shape))


def body(amplitudes, v_plus, v_minus, occ_irrep, col_irrep, block_map):
    rows, depth = amplitudes.shape
    width = v_plus.shape[1]
    orbitals = occ_irrep.shape[0]
    groups = lax.axis_size("x") * lax.axis_size("zh")
    own = orbitals // groups
    slabs = lax.axis_size("y") * lax.axis_size("zl")
    place = jnp.stack([lax.axis_index(("x", "zh")), lax.axis_index("c")]).astype(jnp.int32)
    half = [
        jax.ShapeDtypeStruct((slabs, rows, LANES), F32),
        jax.ShapeDtypeStruct((slabs, rows, LANES), BF16),
    ]
    masked = jax.ShapeDtypeStruct((rows, depth), BF16)
    half_specs = [pl.BlockSpec((1, rows, LANES), lambda s, *_: (s, 0, 0))] * 2
    slab_spec = pl.BlockSpec((depth, 2 * LANES), lambda s, *_: (0, s))
    smem = pl.BlockSpec(memory_space=pltpu.SMEM)
    params = pltpu.CompilerParams(vmem_limit_bytes=48 * MIB)
    cost = pl.CostEstimate(
        flops=2 * rows * depth * width, bytes_accessed=20 * MIB, transcendentals=0
    )
    v_keep, v_send, tm = pl.pallas_call(
        v_kernel,
        grid=(slabs,),
        in_specs=[smem, smem, smem, whole((orbitals, 1)), whole((1, depth)), whole((rows, depth)), slab_spec, slab_spec],
        out_specs=half_specs + [whole((rows, depth))],
        out_shape=half + [masked],
        compiler_params=params,
        cost_estimate=cost,
    )(place, occ_irrep, block_map, occ_irrep.reshape(orbitals, 1), col_irrep.reshape(1, depth), amplitudes, v_plus, v_minus)
    cores = [(0, 1), (1, 0)]
    v_got = lax.ppermute(v_send, "c", cores)
    v_part = (v_keep + v_got.astype(F32)).astype(BF16)
    v_all = lax.all_to_all(
        v_part.reshape(slabs * groups, rows // groups, LANES), ("y", "zl", "x", "zh"), 0, 0, tiled=True
    )

    u_keep, u_send = pl.pallas_call(
        u_kernel,
        grid=(slabs,),
        in_specs=[smem, whole((rows, depth)), slab_spec, slab_spec],
        out_specs=half_specs,
        out_shape=half,
        compiler_params=params,
        cost_estimate=cost,
    )(place, tm, v_plus, v_minus)
    u_got = lax.ppermute(u_send, "c", cores)
    u_part = (u_keep + u_got.astype(F32)).astype(BF16)
    u_all = lax.all_to_all(u_part, ("y", "zl"), 0, 0, tiled=True)

    return pl.pallas_call(
        functools.partial(last_kernel, own),
        out_shape=jax.ShapeDtypeStruct((LANES, rows), BF16),
        scratch_shapes=[pltpu.VMEM((rows, LANES), F32)],
        compiler_params=pltpu.CompilerParams(vmem_limit_bytes=24 * MIB),
    )(u_all, v_all.reshape(slabs, rows, LANES))


def solution(mesh):
    axes = ("x", "zh", "y", "zl", "c")
    fine = Mesh(mesh.devices.reshape(4, 2, 4, 2, 2), axes)
    pair, ctr = ("x", "zh"), ("y", "zl", "c")
    in_specs = (P(pair, ctr), P(ctr, None), P(ctr, None), P(), P(ctr), P())
    return jax.shard_map(body, mesh=fine, in_specs=in_specs, out_specs=P(ctr, pair), check_vma=False)
```

time: 168 us -> 82.5 us (0.49)
  blocking collectives: 97.9 us -> 26.8 us
  Pallas kernels: 0 us -> 24.7 us
  matrix products: 22.7 us -> 0 us
  waiting for transfers between devices: 30.3 us -> 16.1 us
  local copies, waits for them, and re-layouts: 7.59 us -> 2.78 us
  other arithmetic: 0.59 us -> 3.66 us
    psum x1 -> x0, blocking collectives: 97.9 us -> none  [body(): summed = lax.psum(0.5 * (first + second), 'ctr')]
    all_to_all x0 -> x1, blocking collectives: none -> 26.8 us  [body(): lax.all_to_all(v_part.reshape(slabs * groups, rows // groups, LANES), ('y...]
    pallas_call x0 -> x3, Pallas kernels: none -> 24.7 us  [the longest x1 13.1 us: body(): pl.pallas_call(v_kernel, grid=(slabs,), in_specs=[smem, smem, smem, whole...]
    dot_general x3 -> x0, matrix products: 22.7 us -> none  [the longest x1 9.61 us: body(): lax.dot_general(v_minus, anti, dims, preferred_element_type=jnp.float32)]
    all_to_all x1, waiting for transfers between devices: 30.3 us -> 13.3 us  [body(): u_all = lax.all_to_all(u_part, ('y', 'zl'), 0, 0, tiled=True)]
    reshape x1, local copies, waits for them, and re-layouts: 4.26 us -> 0.74 us  [body(): occ_irrep.reshape(orbitals, 1)]
    convert_element_type x1 -> x2, other arithmetic: 0.51 us -> 3.59 us  [the longest x1 2.42 us: body(): v_part = (v_keep + v_got.astype(F32)).astype(BF16)]
    convert_element_type x3 -> x0, local copies, waits for them, and re-layouts: 3.02 us -> none  [the longest x1 2.2 us: body(): par_f = partner.astype(jnp.float32)]
  transfers between devices with their start and end apart: 1 -> 3, of which waited for: 1 -> 2; matrix products, arithmetic and copies ran while one was open for 0% -> 4% of each run, Pallas kernels for 0% -> 0%
where the time goes in v1:
time: 82.5 us; the launch traced here: 81.3 us
  blocking collectives  26.8 us (32%)
  Pallas kernels  24.7 us (30%)
  waiting for transfers between devices  16.1 us (20%)
  starting transfers between devices  7.22 us (9%)
  other arithmetic  3.66 us (4%)
  local copies, waits for them, and re-layouts  2.78 us (3%)
    all_to_all x1, blocking collectives, body(): lax.all_to_all(v_part.reshape(slabs * groups, rows // groups, LANES), ('y...  26.8 us
    all_to_all x1, waiting for transfers between devices, body(): u_all = lax.all_to_all(u_part, ('y', 'zl'), 0, 0, tiled=True)  13.3 us
    pallas_call x1, Pallas kernels, body(): pl.pallas_call(v_kernel, grid=(slabs,), in_specs=[smem, smem, smem, whole...  13.1 us
    pallas_call x1, Pallas kernels, body(): pl.pallas_call(u_kernel, grid=(slabs,), in_specs=[smem, whole((rows, dept...  10.6 us
    all_to_all x1, starting transfers between devices, body(): u_all = lax.all_to_all(u_part, ('y', 'zl'), 0, 0, tiled=True)  5.63 us
    ppermute x1, waiting for transfers between devices, body(): u_got = lax.ppermute(u_send, 'c', cores)  2.76 us
    convert_element_type x1, other arithmetic, body(): v_part = (v_keep + v_got.astype(F32)).astype(BF16)  2.42 us
    unnamed x6, local copies, waits for them, and re-layouts  2.04 us
  transfers between devices with their start and end apart: 3, of which 2 were waited for; matrix products, arithmetic and copies ran while one was open for 4% of the time, Pallas kernels for 0%

profile of v1, /device:TPU:1, one launch (start us, length us, event | category | flops | bytes accessed | tf_op | source)
XLA Modules:
  0.0 81.3 jit_solution(16349994105703508784)
XLA Ops:
  0.0 0.7 copy.7.occ_col_ref
  0.7 0.1 pad_add_fusion.where_ref
  0.8 0.0 copy-start
  0.8 0.7 copy-done
  1.5 0.0 copy-start.1
  1.5 0.7 copy-done.1
  2.2 0.0 copy-start.2
  2.2 0.7 copy-done.2
  2.9 13.1 %shard_map.64 = (f32[8,512,128]{2,1,0:T(8,128)S(1)}, bf16[8,512,128]{2,1,0:T(8,128)(2,1)}, bf16[512,2048]{1,0:T(8,128)(2,1)S(1)}) custom-call(s32[2]{0:T(128)S(1)} %pad_add_fusion.where_ref, s32[64]{0:T(128)S(1)} %copy-done.2, s32[8,8]{1,0:T(8,128)S(1)} %copy-done.1, s32[64,1]{1,0:T(8,128)S(1)} %copy.7.occ_col_ref, s32[1,2048]{1,0:T(1,128)S(1)} %bitcast.7, ...), custom_call_target="tpu_custom_call" | custom-call | flops 4294967296 | bytes 20971520 | tf_op jit(solution)/shard_map/pallas_call | solution.py:103
  16.0 10.6 %shard_map.65 = (f32[8,512,128]{2,1,0:T(8,128)S(1)}, bf16[8,512,128]{2,1,0:T(8,128)(2,1)S(1)}) custom-call(s32[2]{0:T(128)S(1)} %pad_add_fusion.where_ref, bf16[512,2048]{1,0:T(8,128)(2,1)S(1)} %get-tuple-element.10.tm_ref, bf16[2048,2048]{1,0:T(8,128)(2,1)} %p_ref.3, bf16[2048,2048]{1,0:T(8,128)(2,1)} %m_ref.3), custom_call_target="tpu_custom_call" | custom-call | flops 4294967296 | bytes 20971520 | tf_op jit(solution)/shard_map/pallas_call | solution.py:119
  26.6 1.5 %collective-permute-start = (bf16[8,512,128]{2,1,0:T(8,128)(2,1)S(1)}, bf16[8,512,128]{2,1,0:T(8,128)(2,1)S(1)}, u32[]{:S(2)}, u32[]{:S(2)}) collective-permute-start(bf16[8,512,128]{2,1,0:T(8,128)(2,1)S(1)} %get-tuple-element.12), channel_id=1, source_target_pairs={{0,1},{1,0},{2,3},{3,2},{4,5},{5,4},{6,7},{7,6},{8,9},{9,8},{10,11... | collective-permute-start | bytes 3145736 | tf_op jit(solution)/shard_map/ppermute | solution.py:128
  28.1 0.1 collective-permute-start.1
  28.2 2.8 %collective-permute-done = bf16[8,512,128]{2,1,0:T(8,128)(2,1)S(1)} collective-permute-done((bf16[8,512,128]{2,1,0:T(8,128)(2,1)S(1)}, bf16[8,512,128]{2,1,0:T(8,128)(2,1)S(1)}, u32[]{:S(2)}, u32[]{:S(2)}) %collective-permute-start) | collective-permute-done | bytes 1048608 | tf_op jit(solution)/shard_map/ppermute | solution.py:128
  30.9 1.2 %add_convert_fusion.1 = bf16[8,512,128]{2,1,0:T(8,128)(2,1)} fusion(f32[8,512,128]{2,1,0:T(8,128)S(1)} %get-tuple-element.11, bf16[8,512,128]{2,1,0:T(8,128)(2,1)S(1)} %collective-permute-done), kind=kLoop, calls=%fused_computation.1 | loop fusion | flops 1572864 | bytes 4194304 | tf_op jit(solution)/shard_map/convert_element_type | solution.py:129
  32.1 5.6 %all-to-all-start = ((bf16[8,512,128]{2,1,0:T(8,128)(2,1)}), bf16[8,512,128]{2,1,0:T(8,128)(2,1)S(1)}, u32[]{:S(2)}, u32[]{:S(2)}) async-start(bf16[8,512,128]{2,1,0:T(8,128)(2,1)} %add_convert_fusion.1), calls=%async_computation | async-start | bytes 2097152 | tf_op jit(solution)/shard_map/all_to_all | solution.py:130
  37.7 0.0 collective-permute-done.1
  37.7 2.4 %add_convert_fusion = bf16[8,512,128]{2,1,0:T(8,128)(2,1)} fusion(f32[8,512,128]{2,1,0:T(8,128)S(1)} %get-tuple-element.13, bf16[8,512,128]{2,1,0:T(8,128)(2,1)} %collective-permute-done.1), kind=kLoop, calls=%fused_computation | loop fusion | flops 1572864 | bytes 4194304 | tf_op jit(solution)/shard_map/convert_element_type | solution.py:114
  40.2 13.3 %all-to-all-done.u_ref = bf16[8,512,128]{2,1,0:T(8,128)(2,1)S(1)} async-done(((bf16[8,512,128]{2,1,0:T(8,128)(2,1)}), bf16[8,512,128]{2,1,0:T(8,128)(2,1)S(1)}, u32[]{:S(2)}, u32[]{:S(2)}) %all-to-all-start) | async-done | bytes 1048608 | tf_op jit(solution)/shard_map/all_to_all | solution.py:130
  53.4 26.8 %all_to_all.10 = bf16[64,64,128]{2,1,0:T(8,128)(2,1)S(1)} all-to-all(bf16[64,64,128]{2,1,0:T(8,128)(2,1)} %bitcast.9), channel_id=1, replica_groups=mesh['x'=4,'zh'=2,'y'=4,'zl'=2,'c'=2] {'y','zl','x','zh'}, dimensions={0} | all-to-all | bytes 2097152 | tf_op jit(solution)/shard_map/all_to_all | solution.py:115
  80.3 1.0 %shard_map.66 = bf16[128,512]{1,0:T(8,128)(2,1)} custom-call(bf16[8,512,128]{2,1,0:T(8,128)(2,1)S(1)} %all-to-all-done.u_ref, bf16[8,512,128]{2,1,0:T(8,128)(2,1)S(1)} %bitcast.6), custom_call_target="tpu_custom_call" | custom-call | tf_op jit(solution)/shard_map/pallas_call | solution.py:132
Async XLA Ops:
  0.8 0.7 copy-start
  1.5 0.7 copy-start.1
  2.2 0.7 copy-start.2
  26.6 4.4 %collective-permute-start = (bf16[8,512,128]{2,1,0:T(8,128)(2,1)S(1)}, bf16[8,512,128]{2,1,0:T(8,128)(2,1)S(1)}, u32[]{:S(2)}, u32[]{:S(2)}) collective-permute-start(bf16[8,512,128]{2,1,0:T(8,128)(2,1)S(1)} %get-tuple-element.12), channel_id=1, source_target_pairs={{0,1},{1,0},{2,3},{3,2},{4,5},{5,4},{6,7},{7,6},{8,9},{9,8},{10,11... | collective-permute-start | bytes 3145736 | tf_op jit(solution)/shard_map/ppermute | solution.py:128
  28.1 9.7 %collective-permute-start.1 = (bf16[8,512,128]{2,1,0:T(8,128)(2,1)}, bf16[8,512,128]{2,1,0:T(8,128)(2,1)}, u32[]{:S(2)}, u32[]{:S(2)}) collective-permute-start(bf16[8,512,128]{2,1,0:T(8,128)(2,1)} %get-tuple-element.14), channel_id=1, source_target_pairs={{0,1},{1,0},{2,3},{3,2},{4,5},{5,4},{6,7},{7,6},{8,9},{9,8},{10,11... | collective-permute-start | bytes 3145736 | tf_op jit(solution)/shard_map/ppermute | solution.py:113
  32.1 21.3 %all-to-all-start = ((bf16[8,512,128]{2,1,0:T(8,128)(2,1)}), bf16[8,512,128]{2,1,0:T(8,128)(2,1)S(1)}, u32[]{:S(2)}, u32[]{:S(2)}) async-start(bf16[8,512,128]{2,1,0:T(8,128)(2,1)} %add_convert_fusion.1), calls=%async_computation | async-start | bytes 2097152 | tf_op jit(solution)/shard_map/all_to_all | solution.py:130

commit v2 on v0

v2 whole, which is shorter than its diff:
```python
import functools

import jax
import jax.numpy as jnp
from jax import lax
from jax.experimental import pallas as pl
from jax.experimental.pallas import tpu as pltpu
from jax.sharding import Mesh, PartitionSpec as P

F32, BF16, I32 = jnp.float32, jnp.bfloat16, jnp.int32
LANES = 128
MIB = 1 << 20


def across(column, width):
    return jnp.broadcast_to(column, (column.shape[0], width))


def mask_rows(me, occ_ref, map_ref, col_ref, t_ref, tm_ref, label_ref):
    orbitals = occ_ref.shape[1]
    rows, depth = t_ref.shape
    own = rows // orbitals
    irreps = map_ref.shape[0]
    square = (orbitals, orbitals)
    diagonal = lax.broadcasted_iota(I32, square, 0) == lax.broadcasted_iota(I32, square, 1)
    labels = jnp.where(diagonal, jnp.broadcast_to(occ_ref[...], square), 0)
    label_ref[...] = across(jnp.sum(labels, axis=1, keepdims=True), LANES)
    weights = jnp.left_shift(1, lax.broadcasted_iota(I32, map_ref.shape, 1))
    kept = across(jnp.sum(map_ref[...] * weights, axis=1, keepdims=True), LANES)
    col = col_ref[...]
    for a in range(own):
        pair = label_ref[...] ^ label_ref[pl.ds(me * own + a, 1), :]
        word = jnp.zeros_like(pair)
        for r in range(irreps):
            word = jnp.where(pair == r, kept[r : r + 1, :], word)
        word = jnp.concatenate([word] * (depth // LANES), axis=1)
        keep = jnp.right_shift(word, col) & 1
        part = pl.ds(a * orbitals, orbitals)
        tm_ref[part, :] = jnp.where(keep == 1, t_ref[part, :].astype(F32), 0.0).astype(BF16)


def main_kernel(
    occ_hbm, map_hbm, col_hbm, t_hbm, p_hbm, m_hbm,
    vk_hbm, vs_hbm, uk_hbm, us_hbm,
    occ_ref, map_ref, col_ref, label_ref, t_ref, tm_ref, p_ref, m_ref, vk_ref, vs_ref, uk_ref, us_ref,
    small_sem, p_sem, m_sem, out_sem,
):
    slabs = p_ref.shape[0]
    groups = vk_ref.shape[1]
    rows = t_ref.shape[0]
    own = vk_ref.shape[2] // groups
    me = lax.axis_index("x") * lax.axis_size("zh") + lax.axis_index("zh")
    y, zl, core = lax.axis_index("y"), lax.axis_index("zl"), lax.axis_index("c")

    small = [
        pltpu.make_async_copy(src, dst, small_sem.at[i])
        for i, (src, dst) in enumerate(((occ_hbm, occ_ref), (map_hbm, map_ref), (col_hbm, col_ref), (t_hbm, t_ref)))
    ]
    for copy in small:
        copy.start()

    def columns(s):
        return pl.ds(pl.multiple_of(s * 2 * LANES, 2 * LANES), 2 * LANES)

    def loads(s):
        return (
            pltpu.make_async_copy(p_hbm.at[:, columns(s)], p_ref.at[s], p_sem.at[s]),
            pltpu.make_async_copy(m_hbm.at[:, columns(s)], m_ref.at[s], m_sem.at[s]),
        )

    def start(s, carry):
        for copy in loads(s):
            copy.start()
        return carry

    lax.fori_loop(0, slabs, start, 0)
    for copy in small:
        copy.wait()
    mask_rows(me, occ_ref, map_ref, col_ref, t_ref, tm_ref, label_ref)

    half = rows // 2

    def stores(s):
        ys, zs = s // 2, s % 2
        z_slot = jnp.where(zs == zl, 0, 1)
        near, far = y ^ 1, 3 - y
        slot_a = jnp.where(ys == y, 0, jnp.where(ys == far, 1, jnp.where(ys == near, 2, 3)))
        slot_b = jnp.where(ys == y, 0, jnp.where(ys == near, 1, jnp.where(ys == far, 2, 3)))
        first, second = pl.ds(0, half), pl.ds(half, half)
        pairs = (
            (vk_ref.at[s], vk_hbm.at[:, s]),
            (vs_ref.at[s], vs_hbm.at[:, s]),
            (uk_ref.at[s, first], uk_hbm.at[0, slot_a, z_slot]),
            (uk_ref.at[s, second], uk_hbm.at[1, slot_b, z_slot]),
            (us_ref.at[s, first], us_hbm.at[0, slot_a, z_slot]),
            (us_ref.at[s, second], us_hbm.at[1, slot_b, z_slot]),
        )
        return [pltpu.make_async_copy(src, dst, out_sem.at[i, s]) for i, (src, dst) in enumerate(pairs)]

    def by_group(x):
        return jnp.swapaxes(x.reshape(own, groups, own, LANES), 0, 1).reshape(groups, own * own, LANES)

    def step(s, carry):
        for copy in loads(s):
            copy.wait()
        first = jnp.dot(tm_ref[...], p_ref[s], preferred_element_type=F32)
        second = jnp.dot(tm_ref[...], m_ref[s], preferred_element_type=F32)
        u, v = first + second, first - second
        u_low, u_high, v_low, v_high = u[:, :LANES], u[:, LANES:], v[:, :LANES], v[:, LANES:]
        uk_ref[s] = jnp.where(core == 0, u_low, u_high)
        us_ref[s] = jnp.where(core == 0, u_high, u_low).astype(BF16)
        vk_ref[s] = by_group(jnp.where(core == 0, v_low, v_high))
        vs_ref[s] = by_group(jnp.where(core == 0, v_high, v_low)).astype(BF16)
        for copy in stores(s):
            copy.start()
        return carry

    lax.fori_loop(0, slabs, step, 0)

    def finish(s, carry):
        for copy in stores(s):
            copy.wait()
        return carry

    lax.fori_loop(0, slabs, finish, 0)


def last_kernel(own, u_ref, got_ref, v_ref, out_ref, scratch):
    groups, slabs, block, _ = v_ref.shape
    for g in range(groups):
        v = v_ref[g, 0].astype(F32)
        for s in range(1, slabs):
            v = v + v_ref[g, s].astype(F32)
        scratch[pl.ds(g * block, block), :] = v
    orbitals = groups * own
    parts = [scratch[pl.ds(b, orbitals, stride=own), :] for b in range(own)]
    u = (u_ref[...] + got_ref[...].astype(F32)).reshape(groups * block, LANES)
    total = 0.5 * (u + jnp.concatenate(parts, axis=0))
    out_ref[...] = total.T.astype(BF16)


def body(amplitudes, v_plus, v_minus, occ_irrep, col_irrep, block_map):
    rows, depth = amplitudes.shape
    width = v_plus.shape[1]
    orbitals = occ_irrep.shape[0]
    groups = lax.axis_size("x") * lax.axis_size("zh")
    own = orbitals // groups
    ys, zs = lax.axis_size("y"), lax.axis_size("zl")
    slabs = ys * zs
    block = rows // groups
    anywhere = pl.BlockSpec(memory_space=pl.ANY)
    v_shape, u_shape = (groups, slabs, block, LANES), (2, ys, zs, rows // 2, LANES)
    v_keep, v_send, u_keep, u_send = pl.pallas_call(
        main_kernel,
        in_specs=[pl.BlockSpec(memory_space=pltpu.HBM)] * 6,
        out_specs=[anywhere] * 4,
        out_shape=[
            jax.ShapeDtypeStruct(v_shape, F32),
            jax.ShapeDtypeStruct(v_shape, BF16),
            jax.ShapeDtypeStruct(u_shape, F32),
            jax.ShapeDtypeStruct(u_shape, BF16),
        ],
        scratch_shapes=[
            pltpu.VMEM((1, orbitals), I32),
            pltpu.VMEM(block_map.shape, I32),
            pltpu.VMEM((1, depth), I32),
            pltpu.VMEM((orbitals, LANES), I32),
            pltpu.VMEM((rows, depth), BF16),
            pltpu.VMEM((rows, depth), BF16),
            pltpu.VMEM((slabs, depth, 2 * LANES), BF16),
            pltpu.VMEM((slabs, depth, 2 * LANES), BF16),
            pltpu.VMEM((slabs, groups, block, LANES), F32),
            pltpu.VMEM((slabs, groups, block, LANES), BF16),
            pltpu.VMEM((slabs, rows, LANES), F32),
            pltpu.VMEM((slabs, rows, LANES), BF16),
            pltpu.SemaphoreType.DMA((4,)),
            pltpu.SemaphoreType.DMA((slabs,)),
            pltpu.SemaphoreType.DMA((slabs,)),
            pltpu.SemaphoreType.DMA((6, slabs)),
        ],
        compiler_params=pltpu.CompilerParams(vmem_limit_bytes=44 * MIB),
        cost_estimate=pl.CostEstimate(flops=4 * rows * depth * width, bytes_accessed=24 * MIB, transcendentals=0),
    )(occ_irrep.reshape(1, orbitals), block_map, col_irrep.reshape(1, depth), amplitudes, v_plus, v_minus)

    cores = [(0, 1), (1, 0)]
    near = [(i, i ^ 1) for i in range(ys)]
    far = [(i, ys - 1 - i) for i in range(ys)]
    v_got = lax.ppermute(v_send, "c", cores)
    v_part = (v_keep + v_got.astype(F32)).astype(BF16)
    v_all = lax.all_to_all(
        v_part.reshape(groups * slabs, block, LANES), ("x", "zh", "y", "zl"), 0, 0, tiled=True
    )

    u_got = lax.ppermute(u_send, "c", cores)
    part = u_keep + u_got.astype(F32)
    out = part[:, 2:4].astype(BF16)
    got = jnp.stack([lax.ppermute(out[0], "y", near), lax.ppermute(out[1], "y", far)])
    part = part[:, 0:2] + got.astype(F32)
    out = part[:, 1].astype(BF16)
    got = jnp.stack([lax.ppermute(out[0], "y", far), lax.ppermute(out[1], "y", near)])
    part = part[:, 0] + got.astype(F32)
    u_last = lax.ppermute(part[:, 1].astype(BF16), "zl", cores)

    return pl.pallas_call(
        functools.partial(last_kernel, own),
        out_shape=jax.ShapeDtypeStruct((LANES, rows), BF16),
        scratch_shapes=[pltpu.VMEM((rows, LANES), F32)],
        compiler_params=pltpu.CompilerParams(vmem_limit_bytes=24 * MIB),
    )(part[:, 0], u_last, v_all.reshape(v_shape))


def solution(mesh):
    axes = ("x", "zh", "y", "zl", "c")
    fine = Mesh(mesh.devices.reshape(4, 2, 4, 2, 2), axes)
    pair, ctr = ("x", "zh"), ("y", "zl", "c")
    in_specs = (P(pair, ctr), P(ctr, None), P(ctr, None), P(), P(ctr), P())
    return jax.shard_map(body, mesh=fine, in_specs=in_specs, out_specs=P(ctr, pair), check_vma=False)
```

time: 168 us -> 62.5 us (0.37)
  blocking collectives: 97.9 us -> 0 us
  matrix products: 22.7 us -> 0 us
  Pallas kernels: 0 us -> 18 us
  waiting for transfers between devices: 30.3 us -> 18.5 us
  starting transfers between devices: 8.16 us -> 17.4 us
  local copies, waits for them, and re-layouts: 7.59 us -> 4.55 us
  other arithmetic: 0.59 us -> 2.9 us
    psum x1 -> x0, blocking collectives: 97.9 us -> none  [body(): summed = lax.psum(0.5 * (first + second), 'ctr')]
    all_to_all x1, waiting for transfers between devices: 30.3 us -> 0.01 us  [body(): lax.all_to_all(v_part.reshape(groups * slabs, block, LANES), ('x', 'zh',...]
    dot_general x3 -> x0, matrix products: 22.7 us -> none  [the longest x1 9.61 us: body(): lax.dot_general(v_minus, anti, dims, preferred_element_type=jnp.float32)]
    ppermute x0 -> x7, waiting for transfers between devices: none -> 18.5 us  [the longest x1 13.7 us: body(): lax.ppermute(out[0], 'y', far)]
    pallas_call x0 -> x2, Pallas kernels: none -> 18 us  [the longest x1 17 us: body(): pl.pallas_call(main_kernel, in_specs=[pl.BlockSpec(memory_space=pltpu.HBM...]
    ppermute x0 -> x7, starting transfers between devices: none -> 8.43 us  [the longest x1 2.3 us: body(): lax.ppermute(out[0], 'y', far)]
    reshape x1 -> x0, local copies, waits for them, and re-layouts: 4.26 us -> none  [body(): blocks = amplitudes.reshape(own, groups, own, depth)]
    unnamed x10 -> x8, local copies, waits for them, and re-layouts: 0.16 us -> 3.63 us
  transfers between devices with their start and end apart: 1 -> 8, of which waited for: 1 -> 3; matrix products, arithmetic and copies ran while one was open for 0% -> 6% of each run, Pallas kernels for 0% -> 0%
where the time goes in v2:
time: 62.5 us; the launch traced here: 61.4 us
  waiting for transfers between devices  18.5 us (30%)
  Pallas kernels  18 us (29%)
  starting transfers between devices  17.4 us (28%)
  local copies, waits for them, and re-layouts  4.55 us (7%)
  other arithmetic  2.9 us (5%)
    pallas_call x1, Pallas kernels, body(): pl.pallas_call(main_kernel, in_specs=[pl.BlockSpec(memory_space=pltpu.HBM...  17 us
    ppermute x1, waiting for transfers between devices, body(): lax.ppermute(out[0], 'y', far)  13.7 us
    all_to_all x1, starting transfers between devices, body(): lax.all_to_all(v_part.reshape(groups * slabs, block, LANES), ('x', 'zh',...  8.99 us
    unnamed x8, local copies, waits for them, and re-layouts  3.63 us
    ppermute x1, waiting for transfers between devices, body(): u_last = lax.ppermute(part[:, 1].astype(BF16), 'zl', cores)  2.63 us
    ppermute x1, starting transfers between devices, body(): lax.ppermute(out[0], 'y', far)  2.3 us
    ppermute x1, waiting for transfers between devices, body(): u_got = lax.ppermute(u_send, 'c', cores)  2.19 us
    ppermute x1, starting transfers between devices, body(): lax.ppermute(out[1], 'y', far)  1.9 us
  transfers between devices with their start and end apart: 8, of which 3 were waited for; matrix products, arithmetic and copies ran while one was open for 6% of the time, Pallas kernels for 0%

profile of v2, /device:TPU:1, one launch (start us, length us, event | category | flops | bytes accessed | tf_op | source)
XLA Modules:
  0.0 61.4 jit_solution(7115538473365905379)
XLA Ops:
  0.0 0.0 copy-start
  0.0 1.6 %copy-done = bf16[512,2048]{1,0:T(8,128)(2,1)S(1)} copy-done((bf16[512,2048]{1,0:T(8,128)(2,1)S(1)}, bf16[512,2048]{1,0:T(8,128)(2,1)}, u32[]{:S(2)}) %copy-start) | copy-done | bytes 2097176
  1.6 0.0 copy-start.1
  1.6 0.7 %copy-done.1 = s32[2048]{0:T(1024)S(1)} copy-done((s32[2048]{0:T(1024)S(1)}, s32[2048]{0:T(1024)}, u32[]{:S(2)}) %copy-start.1) | copy-done | bytes 8216
  2.3 0.0 copy-start.2
  2.3 0.7 %copy-done.2 = s32[8,8]{1,0:T(8,128)S(1)} copy-done((s32[8,8]{1,0:T(8,128)S(1)}, s32[8,8]{1,0:T(8,128)}, u32[]{:S(2)}) %copy-start.2) | copy-done | bytes 280
  3.0 0.0 copy-start.3
  3.0 0.7 %copy-done.3 = s32[64]{0:T(128)S(1)} copy-done((s32[64]{0:T(128)S(1)}, s32[64]{0:T(128)}, u32[]{:S(2)}) %copy-start.3) | copy-done | bytes 280
  3.6 17.0 %shard_map.64 = (f32[8,8,64,128]{3,2,1,0:T(8,128)S(1)}, bf16[8,8,64,128]{3,2,1,0:T(8,128)(2,1)S(1)}, f32[2,4,2,256,128]{4,3,2,1,0:T(8,128)S(1)}, bf16[2,4,2,256,128]{4,3,2,1,0:T(8,128)(2,1)S(1)}) custom-call(s32[1,64]{1,0:T(1,128)S(1)} %bitcast.27, s32[8,8]{1,0:T(8,128)S(1)} %copy-done.2, s32[1,2048]{1,0:T(1,128)S(1)} %bitcast.26, ...), custom_call_target="tpu_custom_call" | custom-call | flops 8589934592 | bytes 25165824 | tf_op jit(solution)/shard_map/pallas_call | solution.py:153
  20.7 1.5 %collective-permute-start = (bf16[2,4,2,256,128]{4,3,2,1,0:T(8,128)(2,1)S(1)}, bf16[2,4,2,256,128]{4,3,2,1,0:T(8,128)(2,1)S(1)}, u32[]{:S(2)}, u32[]{:S(2)}) collective-permute-start(bf16[2,4,2,256,128]{4,3,2,1,0:T(8,128)(2,1)S(1)} %get-tuple-element.10), channel_id=1, source_target_pairs={{0,1},{1,0},{2,3},{3,2},{4,5},{5,4},{6,7},{7,6},{8,9},{9,8},{10,11... | collective-permute-start | bytes 3145736 | tf_op jit(solution)/shard_map/ppermute | solution.py:194
  22.2 0.1 collective-permute-start.6
  22.3 2.2 %collective-permute-done = bf16[2,4,2,256,128]{4,3,2,1,0:T(8,128)(2,1)S(1)} collective-permute-done((bf16[2,4,2,256,128]{4,3,2,1,0:T(8,128)(2,1)S(1)}, bf16[2,4,2,256,128]{4,3,2,1,0:T(8,128)(2,1)S(1)}, u32[]{:S(2)}, u32[]{:S(2)}) %collective-permute-start) | collective-permute-done | bytes 1048608 | tf_op jit(solution)/shard_map/ppermute | solution.py:194
  24.5 0.4 fusion.2
  24.8 0.9 %slice_bitcast_fusion.3 = (bf16[2,2,256,128]{3,2,1,0:T(8,128)(2,1)}, bf16[2,2,256,128]{3,2,1,0:T(8,128)(2,1)}) fusion(bf16[2,4,2,256,128]{4,3,2,1,0:T(8,128)(2,1)S(1)} %get-tuple-element.15), kind=kLoop, calls=%fused_computation.8 | loop fusion | bytes 1048576 | tf_op jit(solution)/shard_map/squeeze | solution.py:197
  25.7 1.4 %collective-permute-start.1 = (bf16[2,2,256,128]{3,2,1,0:T(8,128)(2,1)}, bf16[2,2,256,128]{3,2,1,0:T(8,128)(2,1)S(1)}, u32[]{:S(2)}, u32[]{:S(2)}) collective-permute-start(bf16[2,2,256,128]{3,2,1,0:T(8,128)(2,1)} %get-tuple-element.17), channel_id=1, source_target_pairs={{0,4},{4,0},{8,12},{12,8},{1,5},{5,1},{9,13},{13,9},{2,6},{6,2},{1... | collective-permute-start | bytes 786440 | tf_op jit(solution)/shard_map/ppermute | solution.py:197
  27.1 1.9 %collective-permute-start.2 = (bf16[2,2,256,128]{3,2,1,0:T(8,128)(2,1)}, bf16[2,2,256,128]{3,2,1,0:T(8,128)(2,1)}, u32[]{:S(2)}, u32[]{:S(2)}) collective-permute-start(bf16[2,2,256,128]{3,2,1,0:T(8,128)(2,1)} %get-tuple-element.18), channel_id=1, source_target_pairs={{0,12},{4,8},{8,4},{12,0},{1,13},{5,9},{9,5},{13,1},{2,14},{6,10},... | collective-permute-start | bytes 786440 | tf_op jit(solution)/shard_map/ppermute | solution.py:197
  29.0 0.0 collective-permute-done.6
  29.0 1.4 %add_convert_fusion = bf16[8,8,64,128]{3,2,1,0:T(8,128)(2,1)} fusion(f32[8,8,64,128]{3,2,1,0:T(8,128)S(1)} %get-tuple-element.11, bf16[8,8,64,128]{3,2,1,0:T(8,128)(2,1)S(1)} %collective-permute-done.6), kind=kLoop, calls=%fused_computation | loop fusion | flops 1572864 | bytes 4194304 | tf_op jit(solution)/shard_map/convert_element_type | solution.py:189
  30.4 9.0 %all-to-all-start = ((bf16[64,64,128]{2,1,0:T(8,128)(2,1)}), bf16[64,64,128]{2,1,0:T(8,128)(2,1)S(1)}, u32[]{:S(2)}, u32[]{:S(2)}) async-start(bf16[64,64,128]{2,1,0:T(8,128)(2,1)} %bitcast.28), calls=%async_computation | async-start | bytes 2097152 | tf_op jit(solution)/shard_map/all_to_all | solution.py:190
  39.4 0.0 collective-permute-done.1
  39.4 0.0 collective-permute-done.2
  39.4 1.1 %fusion.1 = (bf16[2,2,2,256,128]{4,3,2,1,0:T(8,128)(2,1)S(1)}, f32[2,2,2,256,128]{4,3,2,1,0:T(8,128)S(1)}) fusion(bf16[1,2,2,256,128]{4,3,2,1,0:T(8,128)(2,1)} %bitcast.5, bf16[1,2,2,256,128]{4,3,2,1,0:T(8,128)(2,1)S(1)} %bitcast.29, f32[2,4,2,256,128]{4,3,2,1,0:T(8,128)S(1)} %get-tuple-element.16), kind=kLoop, calls=%fused_computation.12 | loop fusion | flops 1048576 | bytes 3145728 | tf_op jit(solution)/shard_map/convert.1
  40.5 2.3 %collective-permute-start.3 = (bf16[2,256,128]{2,1,0:T(8,128)(2,1)S(1)}, bf16[2,256,128]{2,1,0:T(8,128)(2,1)S(1)}, u32[]{:S(2)}, u32[]{:S(2)}) collective-permute-start(bf16[2,256,128]{2,1,0:T(8,128)(2,1)S(1)} %get-tuple-element.19), channel_id=1, source_target_pairs={{0,12},{4,8},{8,4},{12,0},{1,13},{5,9},{9,5},{13,1},{2,14},{6,10},... | collective-permute-start | bytes 393224 | tf_op jit(solution)/shard_map/ppermute | solution.py:200
  42.8 0.0 collective-permute-start.4
  42.8 13.7 %collective-permute-done.3 = bf16[2,256,128]{2,1,0:T(8,128)(2,1)S(1)} collective-permute-done((bf16[2,256,128]{2,1,0:T(8,128)(2,1)S(1)}, bf16[2,256,128]{2,1,0:T(8,128)(2,1)S(1)}, u32[]{:S(2)}, u32[]{:S(2)}) %collective-permute-start.3) | collective-permute-done | bytes 131104 | tf_op jit(solution)/shard_map/ppermute | solution.py:200
  56.5 0.0 collective-permute-done.4
  56.5 0.1 copy_add_fusion
  56.6 1.3 %collective-permute-start.5 = (bf16[2,256,128]{2,1,0:T(8,128)(2,1)S(1)}, bf16[2,256,128]{2,1,0:T(8,128)(2,1)S(1)}, u32[]{:S(2)}, u32[]{:S(2)}) collective-permute-start(bf16[2,256,128]{2,1,0:T(8,128)(2,1)S(1)} %fusion), channel_id=1, source_target_pairs={{0,2},{2,0},{1,3},{3,1},{4,6},{6,4},{5,7},{7,5},{8,10},{10,8},{9,1... | collective-permute-start | bytes 393224 | tf_op jit(solution)/shard_map/ppermute | solution.py:202
  57.9 2.6 %collective-permute-done.5.got_ref = bf16[2,256,128]{2,1,0:T(8,128)(2,1)S(1)} collective-permute-done((bf16[2,256,128]{2,1,0:T(8,128)(2,1)S(1)}, bf16[2,256,128]{2,1,0:T(8,128)(2,1)S(1)}, u32[]{:S(2)}, u32[]{:S(2)}) %collective-permute-start.5) | collective-permute-done | bytes 131104 | tf_op jit(solution)/shard_map/ppermute | solution.py:202
  60.5 0.0 all-to-all-done
  60.5 0.9 %shard_map.65 = bf16[128,512]{1,0:T(8,128)(2,1)} custom-call(f32[2,256,128]{2,1,0:T(8,128)S(1)} %slice_bitcast_fusion.1.u_ref, bf16[2,256,128]{2,1,0:T(8,128)(2,1)S(1)} %collective-permute-done.5.got_ref, bf16[8,8,64,128]{3,2,1,0:T(8,128)(2,1)S(1)} %bitcast.25), custom_call_target="tpu_custom_call" | custom-call | tf_op jit(solution)/shard_map/pallas_call | solution.py:204
  (3 shorter events, 0.1 us)
Async XLA Ops:
  0.0 1.6 %copy-start = (bf16[512,2048]{1,0:T(8,128)(2,1)S(1)}, bf16[512,2048]{1,0:T(8,128)(2,1)}, u32[]{:S(2)}) copy-start(bf16[512,2048]{1,0:T(8,128)(2,1)} %t_hbm.1) | copy-start | bytes 6291460
  1.6 0.7 %copy-start.1 = (s32[2048]{0:T(1024)S(1)}, s32[2048]{0:T(1024)}, u32[]{:S(2)}) copy-start(s32[2048]{0:T(1024)} %param.10) | copy-start | bytes 24580
  2.3 0.7 %copy-start.2 = (s32[8,8]{1,0:T(8,128)S(1)}, s32[8,8]{1,0:T(8,128)}, u32[]{:S(2)}) copy-start(s32[8,8]{1,0:T(8,128)} %map_hbm.1) | copy-start | bytes 772
  3.0 0.7 %copy-start.3 = (s32[64]{0:T(128)S(1)}, s32[64]{0:T(128)}, u32[]{:S(2)}) copy-start(s32[64]{0:T(128)} %param.9) | copy-start | bytes 772
  20.7 3.8 %collective-permute-start = (bf16[2,4,2,256,128]{4,3,2,1,0:T(8,128)(2,1)S(1)}, bf16[2,4,2,256,128]{4,3,2,1,0:T(8,128)(2,1)S(1)}, u32[]{:S(2)}, u32[]{:S(2)}) collective-permute-start(bf16[2,4,2,256,128]{4,3,2,1,0:T(8,128)(2,1)S(1)} %get-tuple-element.10), channel_id=1, source_target_pairs={{0,1},{1,0},{2,3},{3,2},{4,5},{5,4},{6,7},{7,6},{8,9},{9,8},{10,11... | collective-permute-start | bytes 3145736 | tf_op jit(solution)/shard_map/ppermute | solution.py:194
  22.2 6.8 %collective-permute-start.6 = (bf16[8,8,64,128]{3,2,1,0:T(8,128)(2,1)S(1)}, bf16[8,8,64,128]{3,2,1,0:T(8,128)(2,1)S(1)}, u32[]{:S(2)}, u32[]{:S(2)}) collective-permute-start(bf16[8,8,64,128]{3,2,1,0:T(8,128)(2,1)S(1)} %get-tuple-element.12), channel_id=1, source_target_pairs={{0,1},{1,0},{2,3},{3,2},{4,5},{5,4},{6,7},{7,6},{8,9},{9,8},{10,11... | collective-permute-start | bytes 3145736 | tf_op jit(solution)/shard_map/ppermute | solution.py:188
  25.7 13.7 %collective-permute-start.1 = (bf16[2,2,256,128]{3,2,1,0:T(8,128)(2,1)}, bf16[2,2,256,128]{3,2,1,0:T(8,128)(2,1)S(1)}, u32[]{:S(2)}, u32[]{:S(2)}) collective-permute-start(bf16[2,2,256,128]{3,2,1,0:T(8,128)(2,1)} %get-tuple-element.17), channel_id=1, source_target_pairs={{0,4},{4,0},{8,12},{12,8},{1,5},{5,1},{9,13},{13,9},{2,6},{6,2},{1... | collective-permute-start | bytes 786440 | tf_op jit(solution)/shard_map/ppermute | solution.py:197
  27.1 12.3 %collective-permute-start.2 = (bf16[2,2,256,128]{3,2,1,0:T(8,128)(2,1)}, bf16[2,2,256,128]{3,2,1,0:T(8,128)(2,1)}, u32[]{:S(2)}, u32[]{:S(2)}) collective-permute-start(bf16[2,2,256,128]{3,2,1,0:T(8,128)(2,1)} %get-tuple-element.18), channel_id=1, source_target_pairs={{0,12},{4,8},{8,4},{12,0},{1,13},{5,9},{9,5},{13,1},{2,14},{6,10},... | collective-permute-start | bytes 786440 | tf_op jit(solution)/shard_map/ppermute | solution.py:197
  30.4 30.1 %all-to-all-start = ((bf16[64,64,128]{2,1,0:T(8,128)(2,1)}), bf16[64,64,128]{2,1,0:T(8,128)(2,1)S(1)}, u32[]{:S(2)}, u32[]{:S(2)}) async-start(bf16[64,64,128]{2,1,0:T(8,128)(2,1)} %bitcast.28), calls=%async_computation | async-start | bytes 2097152 | tf_op jit(solution)/shard_map/all_to_all | solution.py:190
  40.5 16.0 %collective-permute-start.3 = (bf16[2,256,128]{2,1,0:T(8,128)(2,1)S(1)}, bf16[2,256,128]{2,1,0:T(8,128)(2,1)S(1)}, u32[]{:S(2)}, u32[]{:S(2)}) collective-permute-start(bf16[2,256,128]{2,1,0:T(8,128)(2,1)S(1)} %get-tuple-element.19), channel_id=1, source_target_pairs={{0,12},{4,8},{8,4},{12,0},{1,13},{5,9},{9,5},{13,1},{2,14},{6,10},... | collective-permute-start | bytes 393224 | tf_op jit(solution)/shard_map/ppermute | solution.py:200
  42.8 13.7 %collective-permute-start.4 = (bf16[2,256,128]{2,1,0:T(8,128)(2,1)S(1)}, bf16[2,256,128]{2,1,0:T(8,128)(2,1)S(1)}, u32[]{:S(2)}, u32[]{:S(2)}) collective-permute-start(bf16[2,256,128]{2,1,0:T(8,128)(2,1)S(1)} %get-tuple-element.20), channel_id=1, source_target_pairs={{0,4},{4,0},{8,12},{12,8},{1,5},{5,1},{9,13},{13,9},{2,6},{6,2},{1... | collective-permute-start | bytes 393224 | tf_op jit(solution)/shard_map/ppermute | solution.py:200
  56.6 3.9 %collective-permute-start.5 = (bf16[2,256,128]{2,1,0:T(8,128)(2,1)S(1)}, bf16[2,256,128]{2,1,0:T(8,128)(2,1)S(1)}, u32[]{:S(2)}, u32[]{:S(2)}) collective-permute-start(bf16[2,256,128]{2,1,0:T(8,128)(2,1)S(1)} %fusion), channel_id=1, source_target_pairs={{0,2},{2,0},{1,3},{3,1},{4,6},{6,4},{5,7},{7,5},{8,10},{10,8},{9,1... | collective-permute-start | bytes 393224 | tf_op jit(solution)/shard_map/ppermute | solution.py:202

commit v3 on v2

v3 whole, which is shorter than its diff:
```python
import functools

import jax
import jax.numpy as jnp
from jax import lax
from jax.experimental import pallas as pl
from jax.experimental.pallas import tpu as pltpu
from jax.sharding import Mesh, PartitionSpec as P

F32, BF16, I32 = jnp.float32, jnp.bfloat16, jnp.int32
LANES = 128
MIB = 1 << 20


def across(column, width):
    return jnp.broadcast_to(column, (column.shape[0], width))


def mask_rows(me, occ_ref, map_ref, col_ref, t_ref, tm_ref, label_ref):
    orbitals = occ_ref.shape[1]
    rows, depth = t_ref.shape
    own = rows // orbitals
    irreps = map_ref.shape[0]
    square = (orbitals, orbitals)
    diagonal = lax.broadcasted_iota(I32, square, 0) == lax.broadcasted_iota(I32, square, 1)
    labels = jnp.where(diagonal, jnp.broadcast_to(occ_ref[...], square), 0)
    label_ref[...] = across(jnp.sum(labels, axis=1, keepdims=True), LANES)
    weights = jnp.left_shift(1, lax.broadcasted_iota(I32, map_ref.shape, 1))
    kept = across(jnp.sum(map_ref[...] * weights, axis=1, keepdims=True), LANES)
    col = col_ref[...]
    for a in range(own):
        pair = label_ref[...] ^ label_ref[pl.ds(me * own + a, 1), :]
        word = jnp.zeros_like(pair)
        for r in range(irreps):
            word = jnp.where(pair == r, kept[r : r + 1, :], word)
        word = jnp.concatenate([word] * (depth // LANES), axis=1)
        keep = jnp.right_shift(word, col) & 1
        part = pl.ds(a * orbitals, orbitals)
        tm_ref[part, :] = jnp.where(keep == 1, t_ref[part, :].astype(F32), 0.0).astype(BF16)


def main_kernel(
    occ_hbm, map_hbm, col_hbm, t_hbm, p_hbm, m_hbm,
    vk_ref, vs_ref, ua_ref, ub_ref, us_ref,
    occ_ref, map_ref, col_ref, label_ref, t_ref, tm_ref, p_ref, m_ref, small_sem, p_sem, m_sem,
):
    slabs = p_ref.shape[0]
    groups = vk_ref.shape[0]
    rows = t_ref.shape[0]
    half = rows // 2
    own = vk_ref.shape[2] // groups
    me = lax.axis_index("x") * lax.axis_size("zh") + lax.axis_index("zh")
    y, zl, core = lax.axis_index("y"), lax.axis_index("zl"), lax.axis_index("c")

    small = [
        pltpu.make_async_copy(src, dst, small_sem.at[i])
        for i, (src, dst) in enumerate(((occ_hbm, occ_ref), (map_hbm, map_ref), (col_hbm, col_ref), (t_hbm, t_ref)))
    ]
    for copy in small:
        copy.start()

    def columns(s):
        return pl.ds(pl.multiple_of(s * 2 * LANES, 2 * LANES), 2 * LANES)

    def loads(s):
        return (
            pltpu.make_async_copy(p_hbm.at[:, columns(s)], p_ref.at[s], p_sem.at[s]),
            pltpu.make_async_copy(m_hbm.at[:, columns(s)], m_ref.at[s], m_sem.at[s]),
        )

    def start(s, carry):
        for copy in loads(s):
            copy.start()
        return carry

    lax.fori_loop(0, slabs, start, 0)
    for copy in small:
        copy.wait()
    mask_rows(me, occ_ref, map_ref, col_ref, t_ref, tm_ref, label_ref)

    def by_group(x):
        return jnp.swapaxes(x.reshape(own, groups, own, LANES), 0, 1).reshape(groups, own * own, LANES)

    near, far = y ^ 1, 3 - y

    def step(s, carry):
        for copy in loads(s):
            copy.wait()
        first = jnp.dot(tm_ref[...], p_ref[s], preferred_element_type=F32)
        second = jnp.dot(tm_ref[...], m_ref[s], preferred_element_type=F32)
        u, v = first + second, first - second
        u_low, u_high, v_low, v_high = u[:, :LANES], u[:, LANES:], v[:, :LANES], v[:, LANES:]
        vk_ref[:, s] = by_group(jnp.where(core == 0, v_low, v_high))
        vs_ref[:, s] = by_group(jnp.where(core == 0, v_high, v_low)).astype(BF16)
        ys, zs = s // 2, s % 2
        z_slot = jnp.where(zs == zl, 0, 1)
        slot_a = jnp.where(ys == y, 0, jnp.where(ys == far, 1, jnp.where(ys == near, 2, 3)))
        slot_b = jnp.where(ys == y, 0, jnp.where(ys == near, 1, jnp.where(ys == far, 2, 3)))
        u_keep = jnp.where(core == 0, u_low, u_high)
        u_send = jnp.where(core == 0, u_high, u_low).astype(BF16)
        ua_ref[slot_a, z_slot] = u_keep[:half]
        ub_ref[slot_b, z_slot] = u_keep[half:]
        us_ref[0, slot_a, z_slot] = u_send[:half]
        us_ref[1, slot_b, z_slot] = u_send[half:]
        return carry

    lax.fori_loop(0, slabs, step, 0)


def last_kernel(own, *refs):
    *u_refs, v_ref, out_ref, scratch = refs
    groups, slabs, block, _ = v_ref.shape
    for g in range(groups):
        v = v_ref[g, 0].astype(F32)
        for s in range(1, slabs):
            v = v + v_ref[g, s].astype(F32)
        scratch[pl.ds(g * block, block), :] = v
    orbitals = groups * own
    parts = [scratch[pl.ds(b, orbitals, stride=own), :] for b in range(own)]
    count = len(u_refs) // 2
    halves = []
    for refs in (u_refs[:count], u_refs[count:]):
        u = refs[0][...].astype(F32)
        for ref in refs[1:]:
            u = u + ref[...].astype(F32)
        halves.append(u)
    total = 0.5 * (jnp.concatenate(halves, axis=0) + jnp.concatenate(parts, axis=0))
    out_ref[...] = total.T.astype(BF16)


def body(amplitudes, v_plus, v_minus, occ_irrep, col_irrep, block_map):
    rows, depth = amplitudes.shape
    width = v_plus.shape[1]
    orbitals = occ_irrep.shape[0]
    groups = lax.axis_size("x") * lax.axis_size("zh")
    own = orbitals // groups
    ys, zs = lax.axis_size("y"), lax.axis_size("zl")
    slabs = ys * zs
    block = rows // groups
    in_vmem = pl.BlockSpec(memory_space=pltpu.VMEM)
    operands = (occ_irrep.reshape(1, orbitals), block_map, col_irrep.reshape(1, depth), amplitudes, v_plus, v_minus)
    v_shape, u_shape = (groups, slabs, block, LANES), (ys, zs, rows // 2, LANES)
    v_keep, v_send, a_keep, b_keep, u_send = pl.pallas_call(
        main_kernel,
        in_specs=[pl.BlockSpec(memory_space=pltpu.HBM)] * 6,
        out_specs=[in_vmem] * 5,
        out_shape=[
            pltpu.VMEM(v_shape, F32),
            pltpu.VMEM(v_shape, BF16),
            pltpu.VMEM(u_shape, F32),
            pltpu.VMEM(u_shape, F32),
            pltpu.VMEM((2,) + u_shape, BF16),
        ],
        scratch_shapes=[
            pltpu.VMEM((1, orbitals), I32),
            pltpu.VMEM(block_map.shape, I32),
            pltpu.VMEM((1, depth), I32),
            pltpu.VMEM((orbitals, LANES), I32),
            pltpu.VMEM((rows, depth), BF16),
            pltpu.VMEM((rows, depth), BF16),
            pltpu.VMEM((slabs, depth, 2 * LANES), BF16),
            pltpu.VMEM((slabs, depth, 2 * LANES), BF16),
            pltpu.SemaphoreType.DMA((4,)),
            pltpu.SemaphoreType.DMA((slabs,)),
            pltpu.SemaphoreType.DMA((slabs,)),
        ],
        compiler_params=pltpu.CompilerParams(vmem_limit_bytes=40 * MIB),
        cost_estimate=pl.CostEstimate(flops=4 * rows * depth * width, bytes_accessed=24 * MIB, transcendentals=0),
    )(*(pltpu.with_memory_space_constraint(x, pltpu.HBM) for x in operands))

    cores = [(0, 1), (1, 0)]
    near = [(i, i ^ 1) for i in range(ys)]
    far = [(i, ys - 1 - i) for i in range(ys)]
    near_z = [(2 * a + z, 2 * b + 1 - z) for a, b in near for z in range(2)]
    far_z = [(2 * a + z, 2 * b + 1 - z) for a, b in far for z in range(2)]
    yz = ("y", "zl")
    u_got = lax.ppermute(u_send, "c", cores)
    v_got = lax.ppermute(v_send, "c", cores)
    a_all = a_keep + u_got[0].astype(F32)
    b_all = b_keep + u_got[1].astype(F32)
    a_got = lax.ppermute(a_all[2:4].astype(BF16), "y", near)
    b_got = lax.ppermute(b_all[2:4].astype(BF16), "y", far)
    v_part = (v_keep + v_got.astype(F32)).astype(BF16)
    v_all = lax.all_to_all(
        v_part.reshape(groups * slabs, block, LANES), ("x", "zh", "y", "zl"), 0, 0, tiled=True
    )
    terms = []
    for all_, got, one, two in ((a_all, a_got, far, far_z), (b_all, b_got, near, near_z)):
        part = all_[0:2] + got.astype(F32)
        sends = part.astype(BF16)
        terms += [
            part[0, 0],
            lax.ppermute(sends[1, 0], "y", one),
            lax.ppermute(sends[0, 1], "zl", cores),
            lax.ppermute(sends[1, 1], yz, two),
        ]

    return pl.pallas_call(
        functools.partial(last_kernel, own),
        out_shape=jax.ShapeDtypeStruct((LANES, rows), BF16),
        scratch_shapes=[pltpu.VMEM((rows, LANES), F32)],
        compiler_params=pltpu.CompilerParams(vmem_limit_bytes=24 * MIB),
    )(*terms, v_all.reshape(v_shape))


def solution(mesh):
    axes = ("x", "zh", "y", "zl", "c")
    fine = Mesh(mesh.devices.reshape(4, 2, 4, 2, 2), axes)
    pair, ctr = ("x", "zh"), ("y", "zl", "c")
    in_specs = (P(pair, ctr), P(ctr, None), P(ctr, None), P(), P(ctr), P())
    return jax.shard_map(body, mesh=fine, in_specs=in_specs, out_specs=P(ctr, pair), check_vma=False)
```

time: 62.5 us -> 54.4 us (0.87)
  local copies, waits for them, and re-layouts: 4.55 us -> 0.84 us
  Pallas kernels: 18 us -> 14.5 us
  waiting for transfers between devices: 18.5 us -> 15.4 us
  starting transfers between devices: 17.4 us -> 19 us
  other arithmetic: 2.9 us -> 3.61 us
    unnamed x8 -> x0, local copies, waits for them, and re-layouts: 3.63 us -> none
    pallas_call x1, Pallas kernels: 17 us -> 13.5 us  [body(): pl.pallas_call(main_kernel, in_specs=[pl.BlockSpec(memory_space=pltpu.HBM...]
    ppermute x5 -> x8, waiting for transfers between devices: 16.3 us -> 13.2 us  [the longest x2 9.35 us: body(): lax.ppermute(sends[1, 1], yz, two)]
    convert_element_type x0 -> x2, other arithmetic: none -> 2.05 us  [body(): sends = part.astype(BF16)]
    ppermute x5 -> x8, starting transfers between devices: 6.84 us -> 8.4 us  [the longest x2 3.98 us: body(): lax.ppermute(sends[1, 1], yz, two)]
    another operation x2 -> x0, other arithmetic: 1.48 us -> none
    squeeze x3 -> x4, local copies, waits for them, and re-layouts: 0.9 us -> 0.05 us  [the longest x2 0.03 us: body(): sends[1, 1]]
    slice x0 -> x2, local copies, waits for them, and re-layouts: none -> 0.79 us  [the longest x1 0.75 us: body(): a_got = lax.ppermute(a_all[2:4].astype(BF16), 'y', near)]
  transfers between devices with their start and end apart: 8 -> 11, of which waited for: 3 -> 4; matrix products, arithmetic and copies ran while one was open for 6% -> 8% of each run, Pallas kernels for 0% -> 0%
where the time goes in v3:
time: 54.4 us; the launch traced here: 53.4 us
  starting transfers between devices  19 us (35%)
  waiting for transfers between devices  15.4 us (28%)
  Pallas kernels  14.5 us (27%)
  other arithmetic  3.61 us (7%)
  local copies, waits for them, and re-layouts  0.84 us (2%)
    pallas_call x1, Pallas kernels, body(): pl.pallas_call(main_kernel, in_specs=[pl.BlockSpec(memory_space=pltpu.HBM...  13.5 us
    ppermute x2, waiting for transfers between devices, body(): lax.ppermute(sends[1, 1], yz, two)  9.35 us
    all_to_all x1, starting transfers between devices, body(): lax.all_to_all(v_part.reshape(groups * slabs, block, LANES), ('x', 'zh',...  9 us
    ppermute x2, starting transfers between devices, body(): lax.ppermute(sends[1, 1], yz, two)  3.98 us
    ppermute x2, waiting for transfers between devices, body(): lax.ppermute(sends[0, 1], 'zl', cores)  3.81 us
    ppermute x1, waiting for transfers between devices, body(): u_got = lax.ppermute(u_send, 'c', cores)  2.19 us
    convert_element_type x2, other arithmetic, body(): sends = part.astype(BF16)  2.05 us
    ppermute x1, starting transfers between devices, body(): b_got = lax.ppermute(b_all[2:4].astype(BF16), 'y', far)  1.9 us
  transfers between devices with their start and end apart: 11, of which 4 were waited for; matrix products, arithmetic and copies ran while one was open for 8% of the time, Pallas kernels for 0%

profile of v3, /device:TPU:1, one launch (start us, length us, event | category | flops | bytes accessed | tf_op | source)
XLA Modules:
  0.0 53.4 jit_solution(15250622354401796232)
XLA Ops:
  0.0 13.5 %shard_map.64 = (f32[8,8,64,128]{3,2,1,0:T(8,128)S(1)}, bf16[8,8,64,128]{3,2,1,0:T(8,128)(2,1)S(1)}, f32[4,2,256,128]{3,2,1,0:T(8,128)S(1)}, f32[4,2,256,128]{3,...) custom-call(s32[1,64]{1,0:T(1,128)} %bitcast.32, s32[8,8]{1,0:T(8,128)} %map_hbm.1, s32[1,2048]{1,0:T(1,128)} %bitcast.31, ...), custom_call_target="tpu_custom_call" | custom-call | flops 8589934592 | bytes 25165824 | tf_op jit(solution)/shard_map/pallas_call | solution.py:143
  13.5 1.5 %collective-permute-start = (bf16[2,4,2,256,128]{4,3,2,1,0:T(8,128)(2,1)S(1)}, bf16[2,4,2,256,128]{4,3,2,1,0:T(8,128)(2,1)S(1)}, u32[]{:S(2)}, u32[]{:S(2)}) collective-permute-start(bf16[2,4,2,256,128]{4,3,2,1,0:T(8,128)(2,1)S(1)} %get-tuple-element.11), channel_id=1, source_target_pairs={{0,1},{1,0},{2,3},{3,2},{4,5},{5,4},{6,7},{7,6},{8,9},{9,8},{10,11... | collective-permute-start | bytes 3145736 | tf_op jit(solution)/shard_map/ppermute | solution.py:177
  15.0 0.1 collective-permute-start.9
  15.1 2.2 %collective-permute-done = bf16[2,4,2,256,128]{4,3,2,1,0:T(8,128)(2,1)S(1)} collective-permute-done((bf16[2,4,2,256,128]{4,3,2,1,0:T(8,128)(2,1)S(1)}, bf16[2,4,2,256,128]{4,3,2,1,0:T(8,128)(2,1)S(1)}, u32[]{:S(2)}, u32[]{:S(2)}) %collective-permute-start) | collective-permute-done | bytes 1048608 | tf_op jit(solution)/shard_map/ppermute | solution.py:177
  17.3 0.2 convert_add_fusion
  17.5 0.8 %slice.91 = bf16[2,2,256,128]{3,2,1,0:T(8,128)(2,1)} slice(f32[4,2,256,128]{3,2,1,0:T(8,128)S(1)} %get-tuple-element.20), slice={[2:4], [0:2], [0:256], [0:128]} | slice | bytes 524288 | tf_op jit(solution)/shard_map/slice | solution.py:181
  18.3 1.4 %collective-permute-start.1 = (bf16[2,2,256,128]{3,2,1,0:T(8,128)(2,1)}, bf16[2,2,256,128]{3,2,1,0:T(8,128)(2,1)}, u32[]{:S(2)}, u32[]{:S(2)}) collective-permute-start(bf16[2,2,256,128]{3,2,1,0:T(8,128)(2,1)} %slice.91), channel_id=1, source_target_pairs={{0,4},{4,0},{8,12},{12,8},{1,5},{5,1},{9,13},{13,9},{2,6},{6,2},{1... | collective-permute-start | bytes 786440 | tf_op jit(solution)/shard_map/ppermute | solution.py:181
  19.7 1.9 %collective-permute-start.5 = (bf16[2,2,256,128]{3,2,1,0:T(8,128)(2,1)S(1)}, bf16[2,2,256,128]{3,2,1,0:T(8,128)(2,1)}, u32[]{:S(2)}, u32[]{:S(2)}) collective-permute-start(bf16[2,2,256,128]{3,2,1,0:T(8,128)(2,1)S(1)} %slice.90), channel_id=1, source_target_pairs={{0,12},{4,8},{8,4},{12,0},{1,13},{5,9},{9,5},{13,1},{2,14},{6,10},... | collective-permute-start | bytes 786440 | tf_op jit(solution)/shard_map/ppermute | solution.py:182
  21.6 0.0 collective-permute-done.9
  21.6 1.4 %add_convert_fusion = bf16[8,8,64,128]{3,2,1,0:T(8,128)(2,1)} fusion(f32[8,8,64,128]{3,2,1,0:T(8,128)S(1)} %get-tuple-element.13, bf16[8,8,64,128]{3,2,1,0:T(8,128)(2,1)S(1)} %collective-permute-done.9), kind=kLoop, calls=%fused_computation | loop fusion | flops 1572864 | bytes 4194304 | tf_op jit(solution)/shard_map/convert_element_type | solution.py:183
  23.0 9.0 %all-to-all-start = ((bf16[64,64,128]{2,1,0:T(8,128)(2,1)}), bf16[64,64,128]{2,1,0:T(8,128)(2,1)S(1)}, u32[]{:S(2)}, u32[]{:S(2)}) async-start(bf16[64,64,128]{2,1,0:T(8,128)(2,1)} %bitcast.12), calls=%async_computation | async-start | bytes 2097152 | tf_op jit(solution)/shard_map/all_to_all | solution.py:184
  32.0 0.0 collective-permute-done.1
  32.0 1.0 %fusion.1 = (bf16[2,2,256,128]{3,2,1,0:T(8,128)(2,1)S(1)}, f32[2,2,256,128]{3,2,1,0:T(8,128)S(1)}) fusion(bf16[2,2,256,128]{3,2,1,0:T(8,128)(2,1)} %collective-permute-done.1, f32[4,2,256,128]{3,2,1,0:T(8,128)S(1)} %get-tuple-element.20), kind=kLoop, calls=%fused_computation.18 | loop fusion | flops 393216 | bytes 1572864 | tf_op jit(solution)/shard_map/convert_element_type | solution.py:190
  33.0 3.2 %collective-permute-start.4 = (bf16[256,128]{1,0:T(8,128)(2,1)S(1)}, bf16[256,128]{1,0:T(8,128)(2,1)S(1)}, u32[]{:S(2)}, u32[]{:S(2)}) collective-permute-start(bf16[256,128]{1,0:T(8,128)(2,1)S(1)} %get-tuple-element.24), channel_id=1, source_target_pairs={{0,14},{2,12},{4,10},{6,8},{8,6},{10,4},{12,2},{14,0},{1,15},{3,13... | collective-permute-start | bytes 196616 | tf_op jit(solution)/shard_map/ppermute | solution.py:195
  36.2 0.3 collective-permute-start.3
  36.5 0.5 collective-permute-start.2
  37.0 0.0 collective-permute-done.5
  37.0 1.0 %fusion = (bf16[2,2,256,128]{3,2,1,0:T(8,128)(2,1)S(1)}, f32[2,2,256,128]{3,2,1,0:T(8,128)S(1)}) fusion(bf16[2,2,256,128]{3,2,1,0:T(8,128)(2,1)} %collective-permute-done.5, f32[4,2,256,128]{3,2,1,0:T(8,128)S(1)} %get-tuple-element.19), kind=kLoop, calls=%fused_computation.17 | loop fusion | flops 393216 | bytes 1572864 | tf_op jit(solution)/shard_map/convert_element_type | solution.py:190
  38.0 0.8 %collective-permute-start.8 = (bf16[256,128]{1,0:T(8,128)(2,1)S(1)}, bf16[256,128]{1,0:T(8,128)(2,1)S(1)}, u32[]{:S(2)}, u32[]{:S(2)}) collective-permute-start(bf16[256,128]{1,0:T(8,128)(2,1)S(1)} %get-tuple-element.21), channel_id=1, source_target_pairs={{0,6},{2,4},{4,2},{6,0},{8,14},{10,12},{12,10},{14,8},{1,7},{3,5},... | collective-permute-start | bytes 196616 | tf_op jit(solution)/shard_map/ppermute | solution.py:195
  38.8 0.4 collective-permute-start.7
  39.2 9.3 %collective-permute-done.4.refs_3_ = bf16[256,128]{1,0:T(8,128)(2,1)S(1)} collective-permute-done((bf16[256,128]{1,0:T(8,128)(2,1)S(1)}, bf16[256,128]{1,0:T(8,128)(2,1)S(1)}, u32[]{:S(2)}, u32[]{:S(2)}) %collective-permute-start.4) | collective-permute-done | bytes 65568 | tf_op jit(solution)/shard_map/ppermute | solution.py:195
  48.6 0.0 collective-permute-start.6
  48.6 2.4 %collective-permute-done.3.refs_2_ = bf16[256,128]{1,0:T(8,128)(2,1)S(1)} collective-permute-done((bf16[256,128]{1,0:T(8,128)(2,1)S(1)}, bf16[256,128]{1,0:T(8,128)(2,1)S(1)}, u32[]{:S(2)}, u32[]{:S(2)}) %collective-permute-start.3) | collective-permute-done | bytes 65568 | tf_op jit(solution)/shard_map/ppermute | solution.py:194
  51.0 0.0 collective-permute-done.2.refs_1_
  51.0 0.0 collective-permute-done.8.refs_7_
  51.0 1.4 %collective-permute-done.7.refs_6_ = bf16[256,128]{1,0:T(8,128)(2,1)S(1)} collective-permute-done((bf16[256,128]{1,0:T(8,128)(2,1)S(1)}, bf16[256,128]{1,0:T(8,128)(2,1)S(1)}, u32[]{:S(2)}, u32[]{:S(2)}) %collective-permute-start.7) | collective-permute-done | bytes 65568 | tf_op jit(solution)/shard_map/ppermute | solution.py:194
  52.4 0.0 collective-permute-done.6.refs_5_
  52.4 0.0 all-to-all-done
  52.4 1.0 %shard_map.65 = bf16[128,512]{1,0:T(8,128)(2,1)} custom-call(f32[256,128]{1,0:T(8,128)S(1)} %slice_bitcast_fusion.3.refs_0_, bf16[256,128]{1,0:T(8,128)(2,1)S(1)} %collective-permute-done.2.refs_1_, bf16[256,128]{1,0:T(8,128)(2,1)S(1)} %collective-permute-done.3.refs_2_, bf16[256,128]{1,0:T(8,128)(2,1)S(1)} %collective-permute-done.4.refs_3_, ...), custom_call_target="tpu_custom_call" | custom-call | tf_op jit(solution)/shard_map/pallas_call | solution.py:198
  (5 shorter events, 0.1 us)
Async XLA Ops:
  13.5 3.8 %collective-permute-start = (bf16[2,4,2,256,128]{4,3,2,1,0:T(8,128)(2,1)S(1)}, bf16[2,4,2,256,128]{4,3,2,1,0:T(8,128)(2,1)S(1)}, u32[]{:S(2)}, u32[]{:S(2)}) collective-permute-start(bf16[2,4,2,256,128]{4,3,2,1,0:T(8,128)(2,1)S(1)} %get-tuple-element.11), channel_id=1, source_target_pairs={{0,1},{1,0},{2,3},{3,2},{4,5},{5,4},{6,7},{7,6},{8,9},{9,8},{10,11... | collective-permute-start | bytes 3145736 | tf_op jit(solution)/shard_map/ppermute | solution.py:177
  15.0 6.6 %collective-permute-start.9 = (bf16[8,8,64,128]{3,2,1,0:T(8,128)(2,1)S(1)}, bf16[8,8,64,128]{3,2,1,0:T(8,128)(2,1)S(1)}, u32[]{:S(2)}, u32[]{:S(2)}) collective-permute-start(bf16[8,8,64,128]{3,2,1,0:T(8,128)(2,1)S(1)} %get-tuple-element.14), channel_id=1, source_target_pairs={{0,1},{1,0},{2,3},{3,2},{4,5},{5,4},{6,7},{7,6},{8,9},{9,8},{10,11... | collective-permute-start | bytes 3145736 | tf_op jit(solution)/shard_map/ppermute | solution.py:178
  18.3 13.7 %collective-permute-start.1 = (bf16[2,2,256,128]{3,2,1,0:T(8,128)(2,1)}, bf16[2,2,256,128]{3,2,1,0:T(8,128)(2,1)}, u32[]{:S(2)}, u32[]{:S(2)}) collective-permute-start(bf16[2,2,256,128]{3,2,1,0:T(8,128)(2,1)} %slice.91), channel_id=1, source_target_pairs={{0,4},{4,0},{8,12},{12,8},{1,5},{5,1},{9,13},{13,9},{2,6},{6,2},{1... | collective-permute-start | bytes 786440 | tf_op jit(solution)/shard_map/ppermute | solution.py:181
  19.7 17.3 %collective-permute-start.5 = (bf16[2,2,256,128]{3,2,1,0:T(8,128)(2,1)S(1)}, bf16[2,2,256,128]{3,2,1,0:T(8,128)(2,1)}, u32[]{:S(2)}, u32[]{:S(2)}) collective-permute-start(bf16[2,2,256,128]{3,2,1,0:T(8,128)(2,1)S(1)} %slice.90), channel_id=1, source_target_pairs={{0,12},{4,8},{8,4},{12,0},{1,13},{5,9},{9,5},{13,1},{2,14},{6,10},... | collective-permute-start | bytes 786440 | tf_op jit(solution)/shard_map/ppermute | solution.py:182
  23.0 29.5 %all-to-all-start = ((bf16[64,64,128]{2,1,0:T(8,128)(2,1)}), bf16[64,64,128]{2,1,0:T(8,128)(2,1)S(1)}, u32[]{:S(2)}, u32[]{:S(2)}) async-start(bf16[64,64,128]{2,1,0:T(8,128)(2,1)} %bitcast.12), calls=%async_computation | async-start | bytes 2097152 | tf_op jit(solution)/shard_map/all_to_all | solution.py:184
  33.0 15.5 %collective-permute-start.4 = (bf16[256,128]{1,0:T(8,128)(2,1)S(1)}, bf16[256,128]{1,0:T(8,128)(2,1)S(1)}, u32[]{:S(2)}, u32[]{:S(2)}) collective-permute-start(bf16[256,128]{1,0:T(8,128)(2,1)S(1)} %get-tuple-element.24), channel_id=1, source_target_pairs={{0,14},{2,12},{4,10},{6,8},{8,6},{10,4},{12,2},{14,0},{1,15},{3,13... | collective-permute-start | bytes 196616 | tf_op jit(solution)/shard_map/ppermute | solution.py:195
  36.2 14.8 %collective-permute-start.3 = (bf16[256,128]{1,0:T(8,128)(2,1)S(1)}, bf16[256,128]{1,0:T(8,128)(2,1)S(1)}, u32[]{:S(2)}, u32[]{:S(2)}) collective-permute-start(bf16[256,128]{1,0:T(8,128)(2,1)S(1)} %get-tuple-element.25), channel_id=1, source_target_pairs={{0,2},{2,0},{1,3},{3,1},{4,6},{6,4},{5,7},{7,5},{8,10},{10,8},{9,1... | collective-permute-start | bytes 196616 | tf_op jit(solution)/shard_map/ppermute | solution.py:194
  36.5 14.5 %collective-permute-start.2 = (bf16[256,128]{1,0:T(8,128)(2,1)S(1)}, bf16[256,128]{1,0:T(8,128)(2,1)S(1)}, u32[]{:S(2)}, u32[]{:S(2)}) collective-permute-start(bf16[256,128]{1,0:T(8,128)(2,1)S(1)} %get-tuple-element.26), channel_id=1, source_target_pairs={{0,12},{4,8},{8,4},{12,0},{1,13},{5,9},{9,5},{13,1},{2,14},{6,10},... | collective-permute-start | bytes 196616 | tf_op jit(solution)/shard_map/ppermute | solution.py:193
  38.0 13.0 %collective-permute-start.8 = (bf16[256,128]{1,0:T(8,128)(2,1)S(1)}, bf16[256,128]{1,0:T(8,128)(2,1)S(1)}, u32[]{:S(2)}, u32[]{:S(2)}) collective-permute-start(bf16[256,128]{1,0:T(8,128)(2,1)S(1)} %get-tuple-element.21), channel_id=1, source_target_pairs={{0,6},{2,4},{4,2},{6,0},{8,14},{10,12},{12,10},{14,8},{1,7},{3,5},... | collective-permute-start | bytes 196616 | tf_op jit(solution)/shard_map/ppermute | solution.py:195
  38.8 13.6 %collective-permute-start.7 = (bf16[256,128]{1,0:T(8,128)(2,1)S(1)}, bf16[256,128]{1,0:T(8,128)(2,1)S(1)}, u32[]{:S(2)}, u32[]{:S(2)}) collective-permute-start(bf16[256,128]{1,0:T(8,128)(2,1)S(1)} %get-tuple-element.22), channel_id=1, source_target_pairs={{0,2},{2,0},{1,3},{3,1},{4,6},{6,4},{5,7},{7,5},{8,10},{10,8},{9,1... | collective-permute-start | bytes 196616 | tf_op jit(solution)/shard_map/ppermute | solution.py:194
  48.6 3.8 %collective-permute-start.6 = (bf16[256,128]{1,0:T(8,128)(2,1)S(1)}, bf16[256,128]{1,0:T(8,128)(2,1)S(1)}, u32[]{:S(2)}, u32[]{:S(2)}) collective-permute-start(bf16[256,128]{1,0:T(8,128)(2,1)S(1)} %get-tuple-element.23), channel_id=1, source_target_pairs={{0,4},{4,0},{8,12},{12,8},{1,5},{5,1},{9,13},{13,9},{2,6},{6,2},{1... | collective-permute-start | bytes 196616 | tf_op jit(solution)/shard_map/ppermute | solution.py:193

commit v4 on v3

v4 whole, which is shorter than its diff:
```python
import functools

import jax
import jax.numpy as jnp
from jax import lax
from jax.experimental import pallas as pl
from jax.experimental.pallas import tpu as pltpu
from jax.sharding import Mesh, PartitionSpec as P

F32, BF16, I32, I16 = jnp.float32, jnp.bfloat16, jnp.int32, jnp.int16
LANES = 128
MIB = 1 << 20
VMEM = pl.BlockSpec(memory_space=pltpu.VMEM)
HBM = pl.BlockSpec(memory_space=pltpu.HBM)


def across(column, width):
    return jnp.broadcast_to(column, (column.shape[0], width))


def mask_rows(me, occ_ref, map_ref, col_ref, t_ref, tm_ref, label_ref):
    orbitals = occ_ref.shape[1]
    rows, depth = t_ref.shape
    own = rows // orbitals
    irreps = map_ref.shape[0]
    square = (orbitals, orbitals)
    diagonal = lax.broadcasted_iota(I32, square, 0) == lax.broadcasted_iota(I32, square, 1)
    labels = jnp.where(diagonal, jnp.broadcast_to(occ_ref[...], square), 0)
    label_ref[...] = across(jnp.sum(labels, axis=1, keepdims=True), LANES)
    weights = jnp.left_shift(1, lax.broadcasted_iota(I32, map_ref.shape, 1))
    kept = across(jnp.sum(map_ref[...] * weights, axis=1, keepdims=True), LANES)
    bit = jnp.left_shift(1, jnp.broadcast_to(col_ref[...], (16, depth))).astype(I16)
    bit = jnp.concatenate([bit] * (orbitals // 16), axis=0)
    for a in range(own):
        pair = label_ref[...] ^ label_ref[pl.ds(me * own + a, 1), :]
        word = jnp.zeros_like(pair)
        for r in range(irreps):
            word = jnp.where(pair == r, kept[r : r + 1, :], word)
        word = jnp.concatenate([word.astype(I16)] * (depth // LANES), axis=1)
        part = pl.ds(a * orbitals, orbitals)
        tm_ref[part, :] = jnp.where((word & bit) != 0, t_ref[part, :], jnp.zeros((), BF16))


def by_group(x, shape):
    groups, block, _ = shape
    own = block // groups
    return jnp.swapaxes(x.reshape(own, groups, own, LANES), 0, 1).reshape(shape)


def v_kernel(
    occ_hbm, map_hbm, col_hbm, t_hbm, p_hbm, m_hbm,
    keep_ref, send_ref, tm_ref, p_ref, m_ref,
    occ_ref, map_ref, col_ref, label_ref, t_ref, small_sem, p_sem, m_sem,
):
    slabs = p_ref.shape[0]
    groups, _, block, _ = keep_ref.shape
    wide = 2 * LANES
    me = lax.axis_index("x") * lax.axis_size("zh") + lax.axis_index("zh")
    core = lax.axis_index("c")
    small = [
        pltpu.make_async_copy(src, dst, small_sem.at[i])
        for i, (src, dst) in enumerate(((t_hbm, t_ref), (occ_hbm, occ_ref), (map_hbm, map_ref), (col_hbm, col_ref)))
    ]
    for copy in small:
        copy.start()

    def loads(s):
        columns = pl.ds(pl.multiple_of(s * wide, wide), wide)
        return (
            pltpu.make_async_copy(p_hbm.at[:, columns], p_ref.at[s], p_sem.at[s]),
            pltpu.make_async_copy(m_hbm.at[:, columns], m_ref.at[s], m_sem.at[s]),
        )

    def start(s, carry):
        for copy in loads(s):
            copy.start()
        return carry

    lax.fori_loop(0, slabs, start, 0)
    for copy in small:
        copy.wait()
    mask_rows(me, occ_ref, map_ref, col_ref, t_ref, tm_ref, label_ref)
    shape = (groups, block, LANES)

    def step(b, carry):
        weights = []
        for i in range(2):
            for copy in loads(2 * b + i):
                copy.wait()
            weights.append(p_ref[2 * b + i] - m_ref[2 * b + i])
        v = jnp.dot(tm_ref[...], jnp.concatenate(weights, axis=1), preferred_element_type=F32)
        for i in range(2):
            low = v[:, 2 * i * LANES : (2 * i + 1) * LANES]
            high = v[:, (2 * i + 1) * LANES : (2 * i + 2) * LANES]
            keep_ref[:, 2 * b + i] = by_group(jnp.where(core == 0, low, high), shape)
            send_ref[:, 2 * b + i] = by_group(jnp.where(core == 0, high, low), shape).astype(BF16)
        return carry

    lax.fori_loop(0, slabs // 2, step, 0)


def u_kernel(other, tm_ref, p_ref, m_ref, out_ref):
    y, zl, core = lax.axis_index("y"), lax.axis_index("zl"), lax.axis_index("c")
    parity = 1 - core if other else core
    columns = pl.ds(pl.multiple_of(parity * LANES, LANES), LANES)
    near, far = y ^ 1, 3 - y

    def step(b, carry):
        weights = [p_ref[4 * b + i, :, columns] + m_ref[4 * b + i, :, columns] for i in range(4)]
        u = jnp.dot(tm_ref[...], jnp.concatenate(weights, axis=1), preferred_element_type=F32)
        for i in range(4):
            s = 4 * b + i
            ys, zs = s // 2, s % 2
            z_slot = jnp.where(zs == zl, 0, 1)
            y_slot = jnp.where(ys == y, 0, jnp.where(ys == far, 1, jnp.where(ys == near, 2, 3)))
            out_ref[y_slot, z_slot] = u[:, i * LANES : (i + 1) * LANES].astype(out_ref.dtype)
        return carry

    lax.fori_loop(0, p_ref.shape[0] // 4, step, 0)


def v_add_kernel(keep_ref, got_ref, out_ref):
    def step(h, carry):
        out_ref[h] = (keep_ref[h] + got_ref[h].astype(F32)).astype(BF16)
        return carry

    lax.fori_loop(0, out_ref.shape[0], step, 0)


def first_add_kernel(keep_ref, got_ref, out_ref, rest_ref):
    for slot in range(2):
        for z in range(2):
            total = keep_ref[2 + slot, z] + got_ref[2 + slot, z].astype(F32)
            out_ref[slot, z] = total.astype(BF16)
            rest_ref[slot, z] = keep_ref[slot, z] + got_ref[slot, z].astype(F32)


def second_add_kernel(rest_ref, more_ref, mine_ref, *out_refs):
    for ref, (slot, z) in zip((mine_ref, *out_refs), ((0, 0), (1, 1), (1, 0), (0, 1))):
        ref[...] = (rest_ref[slot, z] + more_ref[slot, z].astype(F32)).astype(ref.dtype)


def last_kernel(mine_ref, far_ref, z_ref, both_ref, v_ref, out_ref, scratch):
    groups, slabs, block, _ = v_ref.shape
    own = block // groups
    for g in range(groups):
        v = v_ref[g, 0].astype(F32)
        for s in range(1, slabs):
            v = v + v_ref[g, s].astype(F32)
        scratch[pl.ds(g * block, block), :] = v
    orbitals = groups * own
    parts = [scratch[pl.ds(b, orbitals, stride=own), :] for b in range(own)]
    u = mine_ref[...]
    for ref in (far_ref, z_ref, both_ref):
        u = u + ref[...].astype(F32)
    out_ref[...] = (0.5 * (u + jnp.concatenate(parts, axis=0))).T.astype(BF16)


def held(x):
    return pltpu.with_memory_space_constraint(x, pltpu.VMEM)


def call(kernel, out_shape, *operands, flops=MIB, scratch=()):
    return pl.pallas_call(
        kernel,
        in_specs=[VMEM] * len(operands),
        out_specs=jax.tree.map(lambda _: VMEM, out_shape),
        out_shape=out_shape,
        scratch_shapes=scratch,
        compiler_params=pltpu.CompilerParams(vmem_limit_bytes=8 * MIB),
        cost_estimate=pl.CostEstimate(flops=flops, bytes_accessed=4 * MIB, transcendentals=0),
    )(*operands)


def body(amplitudes, v_plus, v_minus, occ_irrep, col_irrep, block_map):
    rows, depth = amplitudes.shape
    width = v_plus.shape[1]
    orbitals = occ_irrep.shape[0]
    groups = lax.axis_size("x") * lax.axis_size("zh")
    ys, zs = lax.axis_size("y"), lax.axis_size("zl")
    slabs = ys * zs
    block = rows // groups
    operands = (occ_irrep.reshape(1, orbitals), block_map, col_irrep.reshape(1, depth), amplitudes, v_plus, v_minus)
    v_shape, u_shape = (groups, slabs, block, LANES), (ys, zs, rows, LANES)
    wide = (slabs, depth, 2 * LANES)
    flops = rows * depth * width
    v_keep, v_send, tm, p, m = pl.pallas_call(
        v_kernel,
        in_specs=[HBM] * 6,
        out_specs=[VMEM] * 5,
        out_shape=[
            pltpu.VMEM(v_shape, F32),
            pltpu.VMEM(v_shape, BF16),
            pltpu.VMEM((rows, depth), BF16),
            pltpu.VMEM(wide, BF16),
            pltpu.VMEM(wide, BF16),
        ],
        scratch_shapes=[
            pltpu.VMEM((1, orbitals), I32),
            pltpu.VMEM(block_map.shape, I32),
            pltpu.VMEM((1, depth), I32),
            pltpu.VMEM((orbitals, LANES), I32),
            pltpu.VMEM((rows, depth), BF16),
            pltpu.SemaphoreType.DMA((4,)),
            pltpu.SemaphoreType.DMA((slabs,)),
            pltpu.SemaphoreType.DMA((slabs,)),
        ],
        compiler_params=pltpu.CompilerParams(vmem_limit_bytes=12 * MIB),
        cost_estimate=pl.CostEstimate(flops=2 * flops, bytes_accessed=20 * MIB, transcendentals=0),
    )(*(pltpu.with_memory_space_constraint(x, pltpu.HBM) for x in operands))

    def after(x, *others):
        return lax.optimization_barrier((x, *others))[0]

    cores = [(0, 1), (1, 0)]
    near = [(i, i ^ 1) for i in range(ys)]
    far = [(i, ys - 1 - i) for i in range(ys)]
    far_z = [(2 * a + z, 2 * b + 1 - z) for a, b in far for z in range(2)]
    flat = (rows, LANES)
    v_got = lax.ppermute(v_send, "c", cores)
    u_send = call(functools.partial(u_kernel, True), pltpu.VMEM(u_shape, BF16), held(tm), held(p), held(m), flops=flops)
    v_keep = after(v_keep, u_send)
    v_part = call(v_add_kernel, jax.ShapeDtypeStruct(v_shape, BF16), held(v_keep), held(v_got))
    u_got = lax.ppermute(u_send, "c", cores)
    tm = after(tm, v_part)
    u_keep = call(functools.partial(u_kernel, False), pltpu.VMEM(u_shape, F32), held(tm), held(p), held(m), flops=flops)
    u_out, rest = call(
        first_add_kernel,
        [jax.ShapeDtypeStruct((2, zs, *flat), BF16), pltpu.VMEM((2, zs, *flat), F32)],
        held(u_keep), held(u_got),
    )
    u_more = lax.ppermute(u_out, "y", near)
    v_part = after(v_part, rest)
    v_all = lax.all_to_all(
        v_part.reshape(groups * slabs, block, LANES), ("x", "zh", "y", "zl"), 0, 0, tiled=True
    )
    mine, to_both, to_far, to_z = call(
        second_add_kernel,
        [pltpu.VMEM(flat, F32)] + [jax.ShapeDtypeStruct(flat, BF16)] * 3,
        held(rest), u_more, flops=40 << 30,
    )
    return call(
        last_kernel,
        jax.ShapeDtypeStruct((LANES, rows), BF16),
        mine,
        lax.ppermute(to_both, ("y", "zl"), far_z),
        lax.ppermute(to_far, "y", far),
        lax.ppermute(to_z, "zl", cores),
        v_all.reshape(v_shape),
        scratch=[pltpu.VMEM(flat, F32)],
    )


def solution(mesh):
    axes = ("x", "zh", "y", "zl", "c")
    fine = Mesh(mesh.devices.reshape(4, 2, 4, 2, 2), axes)
    pair, ctr = ("x", "zh"), ("y", "zl", "c")
    in_specs = (P(pair, ctr), P(ctr, None), P(ctr, None), P(), P(ctr), P())
    return jax.shard_map(body, mesh=fine, in_specs=in_specs, out_specs=P(ctr, pair), check_vma=False)
```

time: 54.4 us -> 50.7 us (0.932); the launches traced: 53.4 us -> 50.5 us
  other arithmetic: 3.61 us -> 0 us
  Pallas kernels: 14.5 us -> 15.9 us
  local copies, waits for them, and re-layouts: 0.84 us -> 0 us
  waiting for transfers between devices: 15.4 us -> 16 us
    convert_element_type x3 -> x0, other arithmetic: 3.41 us -> none  [the longest x2 2.05 us: body(): sends = part.astype(BF16)]
    ppermute x8 -> x4, waiting for transfers between devices: 13.2 us -> 16 us  [the longest x1 13 us: body(): lax.ppermute(to_both, ('y', 'zl'), far_z)]
    ppermute x8 -> x4, starting transfers between devices: 8.4 us -> 6.09 us  [the longest x1 4.25 us: body(): lax.ppermute(to_both, ('y', 'zl'), far_z)]
    ppermute x1, waiting for transfers between devices: 2.19 us -> 0.01 us  [body(): u_got = lax.ppermute(u_send, 'c', cores)]
    all_to_all x1, starting transfers between devices: 9 us -> 10.8 us  [body(): lax.all_to_all(v_part.reshape(groups * slabs, block, LANES), ('x', 'zh',...]
    pallas_call x2 -> x7, Pallas kernels: 14.5 us -> 15.9 us  [the longest x1 8.43 us: body(): pl.pallas_call(v_kernel, in_specs=[HBM] * 6, out_specs=[VMEM] * 5, out_sh...]
    ppermute x1, starting transfers between devices: 0.09 us -> 1.49 us  [body(): v_got = lax.ppermute(v_send, 'c', cores)]
    ppermute x1, starting transfers between devices: 1.49 us -> 0.1 us  [body(): u_got = lax.ppermute(u_send, 'c', cores)]
  transfers between devices with their start and end apart: 11 -> 7, of which waited for: 4 -> 3; matrix products, arithmetic and copies ran while one was open for 8% -> 0% of each run, Pallas kernels for 0% -> 13%
where the time goes in v4:
time: 50.7 us; the launch traced here: 50.5 us
  starting transfers between devices  18.5 us (36%)
  waiting for transfers between devices  16 us (32%)
  Pallas kernels  15.9 us (31%)
    ppermute x1, waiting for transfers between devices, body(): lax.ppermute(to_both, ('y', 'zl'), far_z)  13 us
    all_to_all x1, starting transfers between devices, body(): lax.all_to_all(v_part.reshape(groups * slabs, block, LANES), ('x', 'zh',...  10.8 us
    pallas_call x1, Pallas kernels, body(): pl.pallas_call(v_kernel, in_specs=[HBM] * 6, out_specs=[VMEM] * 5, out_sh...  8.43 us
    pallas_call x6, Pallas kernels, call(): pl.pallas_call(kernel, in_specs=[VMEM] * len(operands), out_specs=jax.tre...  7.46 us
    ppermute x1, starting transfers between devices, body(): lax.ppermute(to_both, ('y', 'zl'), far_z)  4.25 us
    ppermute x1, waiting for transfers between devices, body(): lax.ppermute(to_far, 'y', far)  2.22 us
    ppermute x1, starting transfers between devices, body(): v_got = lax.ppermute(v_send, 'c', cores)  1.49 us
    ppermute x1, starting transfers between devices, body(): u_more = lax.ppermute(u_out, 'y', near)  1.47 us
  transfers between devices with their start and end apart: 7, of which 3 were waited for; matrix products, arithmetic and copies ran while one was open for 0% of the time, Pallas kernels for 13%

profile of v4, /device:TPU:1, one launch (start us, length us, event | category | flops | bytes accessed | tf_op | source)
XLA Modules:
  0.0 50.5 jit_solution(17310846476857904539)
XLA Ops:
  0.0 8.4 %shard_map.64 = (f32[8,8,64,128]{3,2,1,0:T(8,128)S(1)}, bf16[8,8,64,128]{3,2,1,0:T(8,128)(2,1)S(1)}, bf16[512,2048]{1,0:T(8,128)(2,1)S(1)}, bf16[8,2048,256]{2,1,0:T(8,128)(2,1)S(1)}, bf16[8,2048,256]{2,1,0:T(8,128)(2,1)S(1)}) custom-call(s32[1,64]{1,0:T(1,128)} %bitcast.6, s32[8,8]{1,0:T(8,128)} %map_hbm.1, s32[1,2048]{1,0:T(1,128)} %bitcast.5, ...), custom_call_target="tpu_custom_call" | custom-call | flops 4294967296 | bytes 20971520 | tf_op jit(solution)/shard_map/pallas_call | solution.py:187
  8.4 1.5 %collective-permute-start = (bf16[8,8,64,128]{3,2,1,0:T(8,128)(2,1)S(1)}, bf16[8,8,64,128]{3,2,1,0:T(8,128)(2,1)S(1)}, u32[]{:S(2)}, u32[]{:S(2)}) collective-permute-start(bf16[8,8,64,128]{3,2,1,0:T(8,128)(2,1)S(1)} %get-tuple-element.24), channel_id=1, source_target_pairs={{0,1},{1,0},{2,3},{3,2},{4,5},{5,4},{6,7},{7,6},{8,9},{9,8},{10,11... | collective-permute-start | bytes 3145736 | tf_op jit(solution)/shard_map/ppermute | solution.py:220
  9.9 2.5 %shard_map.65 = bf16[4,2,512,128]{3,2,1,0:T(8,128)(2,1)S(1)} custom-call(bf16[512,2048]{1,0:T(8,128)(2,1)S(1)} %get-tuple-element.25.tm_ref, bf16[8,2048,256]{2,1,0:T(8,128)(2,1)S(1)} %get-tuple-element.21.p_ref, bf16[8,2048,256]{2,1,0:T(8,128)(2,1)S(1)} %get-tuple-element.22.m_ref), custom_call_target="tpu_custom_call" | custom-call | flops 2147483648 | bytes 4194304 | tf_op jit(solution)/shard_map/pallas_call | solution.py:164
  12.5 0.1 collective-permute-start.1
  12.6 0.0 collective-permute-done.got_ref
  12.6 1.2 %shard_map.66 = bf16[8,8,64,128]{3,2,1,0:T(8,128)(2,1)} custom-call(f32[8,8,64,128]{3,2,1,0:T(8,128)S(1)} %get-tuple-element.23.keep_ref, bf16[8,8,64,128]{3,2,1,0:T(8,128)(2,1)S(1)} %collective-permute-done.got_ref), custom_call_target="tpu_custom_call" | custom-call | flops 1048576 | bytes 4194304 | tf_op jit(solution)/shard_map/pallas_call | solution.py:164
  13.8 2.5 %shard_map.67.keep_ref = f32[4,2,512,128]{3,2,1,0:T(8,128)S(1)} custom-call(bf16[512,2048]{1,0:T(8,128)(2,1)S(1)} %get-tuple-element.25.tm_ref, bf16[8,2048,256]{2,1,0:T(8,128)(2,1)S(1)} %get-tuple-element.21.p_ref, bf16[8,2048,256]{2,1,0:T(8,128)(2,1)S(1)} %get-tuple-element.22.m_ref), custom_call_target="tpu_custom_call" | custom-call | flops 2147483648 | bytes 4194304 | tf_op jit(solution)/shard_map/pallas_call | solution.py:164
  16.3 0.0 collective-permute-done.1.got_ref
  16.3 0.2 shard_map.68
  16.5 1.5 %collective-permute-start.2 = (bf16[2,2,512,128]{3,2,1,0:T(8,128)(2,1)S(1)}, bf16[2,2,512,128]{3,2,1,0:T(8,128)(2,1)S(1)}, u32[]{:S(2)}, u32[]{:S(2)}) collective-permute-start(bf16[2,2,512,128]{3,2,1,0:T(8,128)(2,1)S(1)} %get-tuple-element.27), channel_id=1, source_target_pairs={{0,4},{4,0},{8,12},{12,8},{1,5},{5,1},{9,13},{13,9},{2,6},{6,2},{1... | collective-permute-start | bytes 1572872 | tf_op jit(solution)/shard_map/ppermute | solution.py:232
  18.0 10.8 %all-to-all-start = ((bf16[64,64,128]{2,1,0:T(8,128)(2,1)}), bf16[64,64,128]{2,1,0:T(8,128)(2,1)S(1)}, u32[]{:S(2)}, u32[]{:S(2)}) async-start(bf16[64,64,128]{2,1,0:T(8,128)(2,1)} %bitcast.2), calls=%async_computation | async-start | bytes 2097152 | tf_op jit(solution)/shard_map/all_to_all | solution.py:234
  28.8 0.8 %collective-permute-done.2.more_ref = bf16[2,2,512,128]{3,2,1,0:T(8,128)(2,1)S(1)} collective-permute-done((bf16[2,2,512,128]{3,2,1,0:T(8,128)(2,1)S(1)}, bf16[2,2,512,128]{3,2,1,0:T(8,128)(2,1)S(1)}, u32[]{:S(2)}, u32[]{:S(2)}) %collective-permute-start.2) | collective-permute-done | bytes 524320 | tf_op jit(solution)/shard_map/ppermute | solution.py:232
  29.6 0.1 shard_map.69
  29.7 4.3 %collective-permute-start.3 = (bf16[512,128]{1,0:T(8,128)(2,1)S(1)}, bf16[512,128]{1,0:T(8,128)(2,1)S(1)}, u32[]{:S(2)}, u32[]{:S(2)}) collective-permute-start(bf16[512,128]{1,0:T(8,128)(2,1)S(1)} %get-tuple-element.29), channel_id=1, source_target_pairs={{0,14},{2,12},{4,10},{6,8},{8,6},{10,4},{12,2},{14,0},{1,15},{3,13... | collective-permute-start | bytes 393224 | tf_op jit(solution)/shard_map/ppermute | solution.py:246
  33.9 0.0 collective-permute-start.4
  33.9 0.4 collective-permute-start.5
  34.3 13.0 %collective-permute-done.3.far_ref = bf16[512,128]{1,0:T(8,128)(2,1)S(1)} collective-permute-done((bf16[512,128]{1,0:T(8,128)(2,1)S(1)}, bf16[512,128]{1,0:T(8,128)(2,1)S(1)}, u32[]{:S(2)}, u32[]{:S(2)}) %collective-permute-start.3) | collective-permute-done | bytes 131104 | tf_op jit(solution)/shard_map/ppermute | solution.py:246
  47.3 2.2 %collective-permute-done.4.z_ref = bf16[512,128]{1,0:T(8,128)(2,1)S(1)} collective-permute-done((bf16[512,128]{1,0:T(8,128)(2,1)S(1)}, bf16[512,128]{1,0:T(8,128)(2,1)S(1)}, u32[]{:S(2)}, u32[]{:S(2)}) %collective-permute-start.4) | collective-permute-done | bytes 131104 | tf_op jit(solution)/shard_map/ppermute | solution.py:247
  49.5 0.0 collective-permute-done.5.both_ref
  49.5 0.0 all-to-all-done
  49.5 1.0 %shard_map.70 = bf16[128,512]{1,0:T(8,128)(2,1)} custom-call(f32[512,128]{1,0:T(8,128)S(1)} %get-tuple-element.28.mine_ref, bf16[512,128]{1,0:T(8,128)(2,1)S(1)} %collective-permute-done.3.far_ref, bf16[512,128]{1,0:T(8,128)(2,1)S(1)} %collective-permute-done.4.z_ref, bf16[512,128]{1,0:T(8,128)(2,1)S(1)} %collective-permute-done.5.both_ref, ...), custom_call_target="tpu_custom_call" | custom-call | flops 1048576 | bytes 4194304 | tf_op jit(solution)/shard_map/pallas_call | solution.py:164
Async XLA Ops:
  8.4 4.1 %collective-permute-start = (bf16[8,8,64,128]{3,2,1,0:T(8,128)(2,1)S(1)}, bf16[8,8,64,128]{3,2,1,0:T(8,128)(2,1)S(1)}, u32[]{:S(2)}, u32[]{:S(2)}) collective-permute-start(bf16[8,8,64,128]{3,2,1,0:T(8,128)(2,1)S(1)} %get-tuple-element.24), channel_id=1, source_target_pairs={{0,1},{1,0},{2,3},{3,2},{4,5},{5,4},{6,7},{7,6},{8,9},{9,8},{10,11... | collective-permute-start | bytes 3145736 | tf_op jit(solution)/shard_map/ppermute | solution.py:220
  12.5 3.8 %collective-permute-start.1 = (bf16[4,2,512,128]{3,2,1,0:T(8,128)(2,1)S(1)}, bf16[4,2,512,128]{3,2,1,0:T(8,128)(2,1)S(1)}, u32[]{:S(2)}, u32[]{:S(2)}) collective-permute-start(bf16[4,2,512,128]{3,2,1,0:T(8,128)(2,1)S(1)} %shard_map.65), channel_id=1, source_target_pairs={{0,1},{1,0},{2,3},{3,2},{4,5},{5,4},{6,7},{7,6},{8,9},{9,8},{10,11... | collective-permute-start | bytes 3145736 | tf_op jit(solution)/shard_map/ppermute | solution.py:224
  16.5 13.1 %collective-permute-start.2 = (bf16[2,2,512,128]{3,2,1,0:T(8,128)(2,1)S(1)}, bf16[2,2,512,128]{3,2,1,0:T(8,128)(2,1)S(1)}, u32[]{:S(2)}, u32[]{:S(2)}) collective-permute-start(bf16[2,2,512,128]{3,2,1,0:T(8,128)(2,1)S(1)} %get-tuple-element.27), channel_id=1, source_target_pairs={{0,4},{4,0},{8,12},{12,8},{1,5},{5,1},{9,13},{13,9},{2,6},{6,2},{1... | collective-permute-start | bytes 1572872 | tf_op jit(solution)/shard_map/ppermute | solution.py:232
  18.0 31.6 %all-to-all-start = ((bf16[64,64,128]{2,1,0:T(8,128)(2,1)}), bf16[64,64,128]{2,1,0:T(8,128)(2,1)S(1)}, u32[]{:S(2)}, u32[]{:S(2)}) async-start(bf16[64,64,128]{2,1,0:T(8,128)(2,1)} %bitcast.2), calls=%async_computation | async-start | bytes 2097152 | tf_op jit(solution)/shard_map/all_to_all | solution.py:234
  29.7 17.6 %collective-permute-start.3 = (bf16[512,128]{1,0:T(8,128)(2,1)S(1)}, bf16[512,128]{1,0:T(8,128)(2,1)S(1)}, u32[]{:S(2)}, u32[]{:S(2)}) collective-permute-start(bf16[512,128]{1,0:T(8,128)(2,1)S(1)} %get-tuple-element.29), channel_id=1, source_target_pairs={{0,14},{2,12},{4,10},{6,8},{8,6},{10,4},{12,2},{14,0},{1,15},{3,13... | collective-permute-start | bytes 393224 | tf_op jit(solution)/shard_map/ppermute | solution.py:246
  33.9 15.6 %collective-permute-start.4 = (bf16[512,128]{1,0:T(8,128)(2,1)S(1)}, bf16[512,128]{1,0:T(8,128)(2,1)S(1)}, u32[]{:S(2)}, u32[]{:S(2)}) collective-permute-start(bf16[512,128]{1,0:T(8,128)(2,1)S(1)} %get-tuple-element.30), channel_id=1, source_target_pairs={{0,12},{4,8},{8,4},{12,0},{1,13},{5,9},{9,5},{13,1},{2,14},{6,10},... | collective-permute-start | bytes 393224 | tf_op jit(solution)/shard_map/ppermute | solution.py:247
  33.9 15.6 %collective-permute-start.5 = (bf16[512,128]{1,0:T(8,128)(2,1)S(1)}, bf16[512,128]{1,0:T(8,128)(2,1)S(1)}, u32[]{:S(2)}, u32[]{:S(2)}) collective-permute-start(bf16[512,128]{1,0:T(8,128)(2,1)S(1)} %get-tuple-element.31), channel_id=1, source_target_pairs={{0,2},{2,0},{1,3},{3,1},{4,6},{6,4},{5,7},{7,5},{8,10},{10,8},{9,1... | collective-permute-start | bytes 393224 | tf_op jit(solution)/shard_map/ppermute | solution.py:248

commit v5 on v4

--- a/solution.py
+++ b/solution.py
@@ -99,9 +99,8 @@
     lax.fori_loop(0, slabs // 2, step, 0)
 
 
-def u_kernel(other, tm_ref, p_ref, m_ref, out_ref):
-    y, zl, core = lax.axis_index("y"), lax.axis_index("zl"), lax.axis_index("c")
-    parity = 1 - core if other else core
+def u_kernel(parity, tm_ref, p_ref, m_ref, out_ref):
+    y, zl = lax.axis_index("y"), lax.axis_index("zl")
     columns = pl.ds(pl.multiple_of(parity * LANES, LANES), LANES)
     near, far = y ^ 1, 3 - y
 
@@ -119,12 +118,19 @@
     lax.fori_loop(0, p_ref.shape[0] // 4, step, 0)
 
 
-def v_add_kernel(keep_ref, got_ref, out_ref):
-    def step(h, carry):
-        out_ref[h] = (keep_ref[h] + got_ref[h].astype(F32)).astype(BF16)
-        return carry
-
-    lax.fori_loop(0, out_ref.shape[0], step, 0)
+def u_send_kernel(*refs):
+    u_kernel(1 - lax.axis_index("c"), *refs)
+
+
+def u_keep_kernel(tm_ref, p_ref, m_ref, vk_ref, vg_ref, out_ref, v_hbm, v_ref, sem):
+    copies = []
+    for h in range(v_ref.shape[0]):
+        v_ref[h] = (vk_ref[h] + vg_ref[h].astype(F32)).astype(BF16)
+        copies.append(pltpu.make_async_copy(v_ref.at[h], v_hbm.at[h], sem.at[h]))
+        copies[-1].start()
+    u_kernel(lax.axis_index("c"), tm_ref, p_ref, m_ref, out_ref)
+    for copy in copies:
+        copy.wait()
 
 
 def first_add_kernel(keep_ref, got_ref, out_ref, rest_ref):
@@ -218,12 +224,18 @@
     far_z = [(2 * a + z, 2 * b + 1 - z) for a, b in far for z in range(2)]
     flat = (rows, LANES)
     v_got = lax.ppermute(v_send, "c", cores)
-    u_send = call(functools.partial(u_kernel, True), pltpu.VMEM(u_shape, BF16), held(tm), held(p), held(m), flops=flops)
-    v_keep = after(v_keep, u_send)
-    v_part = call(v_add_kernel, jax.ShapeDtypeStruct(v_shape, BF16), held(v_keep), held(v_got))
+    factors = [held(x) for x in (tm, p, m)]
+    u_send = call(u_send_kernel, pltpu.VMEM(u_shape, BF16), *factors, flops=flops)
     u_got = lax.ppermute(u_send, "c", cores)
-    tm = after(tm, v_part)
-    u_keep = call(functools.partial(u_kernel, False), pltpu.VMEM(u_shape, F32), held(tm), held(p), held(m), flops=flops)
+    u_keep, v_part = pl.pallas_call(
+        u_keep_kernel,
+        in_specs=[VMEM] * 5,
+        out_specs=[VMEM, HBM],
+        out_shape=[pltpu.VMEM(u_shape, F32), pltpu.HBM(v_shape, BF16)],
+        scratch_shapes=[pltpu.VMEM(v_shape, BF16), pltpu.SemaphoreType.DMA((groups,))],
+        compiler_params=pltpu.CompilerParams(vmem_limit_bytes=8 * MIB),
+        cost_estimate=pl.CostEstimate(flops=flops, bytes_accessed=4 * MIB, transcendentals=0),
+    )(*factors, held(after(v_keep, u_send)), held(v_got))
     u_out, rest = call(
         first_add_kernel,
         [jax.ShapeDtypeStruct((2, zs, *flat), BF16), pltpu.VMEM((2, zs, *flat), F32)],

time: 50.7 us -> 49.8 us (0.982)
  Pallas kernels: 15.9 us -> 15 us
    pallas_call x6 -> x4, Pallas kernels: 7.46 us -> 3.74 us  [call(): pl.pallas_call(kernel, in_specs=[VMEM] * len(operands), out_specs=jax.tre...]
    pallas_call x0 -> x1, Pallas kernels: none -> 2.8 us  [body(): pl.pallas_call(u_keep_kernel, in_specs=[VMEM] * 5, out_specs=[VMEM, HBM],...]
  transfers between devices with their start and end apart: 7 -> 7, of which waited for: 3 -> 3; matrix products, arithmetic and copies ran while one was open for 0% -> 0% of each run, Pallas kernels for 13% -> 11%
where the time goes in v5:
time: 49.8 us; the launch traced here: 49.5 us
  starting transfers between devices  18.5 us (37%)
  waiting for transfers between devices  16 us (32%)
  Pallas kernels  15 us (30%)
    ppermute x1, waiting for transfers between devices, body(): lax.ppermute(to_both, ('y', 'zl'), far_z)  13 us
    all_to_all x1, starting transfers between devices, body(): lax.all_to_all(v_part.reshape(groups * slabs, block, LANES), ('x', 'zh',...  10.8 us
    pallas_call x1, Pallas kernels, body(): pl.pallas_call(v_kernel, in_specs=[HBM] * 6, out_specs=[VMEM] * 5, out_sh...  8.43 us
    ppermute x1, starting transfers between devices, body(): lax.ppermute(to_both, ('y', 'zl'), far_z)  4.25 us
    pallas_call x4, Pallas kernels, call(): pl.pallas_call(kernel, in_specs=[VMEM] * len(operands), out_specs=jax.tre...  3.74 us
    pallas_call x1, Pallas kernels, body(): pl.pallas_call(u_keep_kernel, in_specs=[VMEM] * 5, out_specs=[VMEM, HBM],...  2.8 us
    ppermute x1, waiting for transfers between devices, body(): lax.ppermute(to_far, 'y', far)  2.21 us
    ppermute x1, starting transfers between devices, body(): v_got = lax.ppermute(v_send, 'c', cores)  1.49 us
  transfers between devices with their start and end apart: 7, of which 3 were waited for; matrix products, arithmetic and copies ran while one was open for 0% of the time, Pallas kernels for 11%

profile of v5, /device:TPU:1, one launch (start us, length us, event | category | flops | bytes accessed | tf_op | source)
XLA Modules:
  0.0 49.5 jit_solution(2695871255189956876)
XLA Ops:
  0.0 8.4 %shard_map.64 = (f32[8,8,64,128]{3,2,1,0:T(8,128)S(1)}, bf16[8,8,64,128]{3,2,1,0:T(8,128)(2,1)S(1)}, bf16[512,2048]{1,0:T(8,128)(2,1)S(1)}, bf16[8,2048,256]{2,1,0:T(8,128)(2,1)S(1)}, bf16[8,2048,256]{2,1,0:T(8,128)(2,1)S(1)}) custom-call(s32[1,64]{1,0:T(1,128)} %bitcast.7, s32[8,8]{1,0:T(8,128)} %map_hbm.1, s32[1,2048]{1,0:T(1,128)} %bitcast.6, ...), custom_call_target="tpu_custom_call" | custom-call | flops 4294967296 | bytes 20971520 | tf_op jit(solution)/shard_map/pallas_call | solution.py:193
  8.4 1.5 %collective-permute-start = (bf16[8,8,64,128]{3,2,1,0:T(8,128)(2,1)S(1)}, bf16[8,8,64,128]{3,2,1,0:T(8,128)(2,1)S(1)}, u32[]{:S(2)}, u32[]{:S(2)}) collective-permute-start(bf16[8,8,64,128]{3,2,1,0:T(8,128)(2,1)S(1)} %get-tuple-element.25), channel_id=1, source_target_pairs={{0,1},{1,0},{2,3},{3,2},{4,5},{5,4},{6,7},{7,6},{8,9},{9,8},{10,11... | collective-permute-start | bytes 3145736 | tf_op jit(solution)/shard_map/ppermute | solution.py:226
  9.9 2.5 %shard_map.65 = bf16[4,2,512,128]{3,2,1,0:T(8,128)(2,1)S(1)} custom-call(bf16[512,2048]{1,0:T(8,128)(2,1)S(1)} %get-tuple-element.20.refs_0_.tm_ref, bf16[8,2048,256]{2,1,0:T(8,128)(2,1)S(1)} %get-tuple-element.21.refs_1_.p_ref, bf16[8,2048,256]{2,1,0:T(8,128)(2,1)S(1)} %get-tuple-element.22.refs_2_.m_ref), custom_call_target="tpu_custom_call" | custom-call | flops 2147483648 | bytes 4194304 | tf_op jit(solution)/shard_map/pallas_call | solution.py:170
  12.5 0.1 collective-permute-start.1
  12.6 0.0 collective-permute-done.vg_ref
  12.6 2.8 %shard_map.66 = (f32[4,2,512,128]{3,2,1,0:T(8,128)S(1)}, bf16[8,8,64,128]{3,2,1,0:T(8,128)(2,1)}) custom-call(bf16[512,2048]{1,0:T(8,128)(2,1)S(1)} %get-tuple-element.20.refs_0_.tm_ref, bf16[8,2048,256]{2,1,0:T(8,128)(2,1)S(1)} %get-tuple-element.21.refs_1_.p_ref, bf16[8,2048,256]{2,1,0:T(8,128)(2,1)S(1)} %get-tuple-element.22.refs_2_.m_ref, ...), custom_call_target="tpu_custom_call" | custom-call | flops 2147483648 | bytes 4194304 | tf_op jit(solution)/shard_map/pallas_call | solution.py:230
  15.4 0.0 collective-permute-done.1.got_ref
  15.4 0.2 shard_map.67
  15.6 1.5 %collective-permute-start.2 = (bf16[2,2,512,128]{3,2,1,0:T(8,128)(2,1)S(1)}, bf16[2,2,512,128]{3,2,1,0:T(8,128)(2,1)S(1)}, u32[]{:S(2)}, u32[]{:S(2)}) collective-permute-start(bf16[2,2,512,128]{3,2,1,0:T(8,128)(2,1)S(1)} %get-tuple-element.28), channel_id=1, source_target_pairs={{0,4},{4,0},{8,12},{12,8},{1,5},{5,1},{9,13},{13,9},{2,6},{6,2},{1... | collective-permute-start | bytes 1572872 | tf_op jit(solution)/shard_map/ppermute | solution.py:244
  17.0 10.8 %all-to-all-start = ((bf16[64,64,128]{2,1,0:T(8,128)(2,1)}), bf16[64,64,128]{2,1,0:T(8,128)(2,1)S(1)}, u32[]{:S(2)}, u32[]{:S(2)}) async-start(bf16[64,64,128]{2,1,0:T(8,128)(2,1)} %bitcast.5), calls=%async_computation | async-start | bytes 2097152 | tf_op jit(solution)/shard_map/all_to_all | solution.py:246
  27.9 0.8 %collective-permute-done.2.more_ref = bf16[2,2,512,128]{3,2,1,0:T(8,128)(2,1)S(1)} collective-permute-done((bf16[2,2,512,128]{3,2,1,0:T(8,128)(2,1)S(1)}, bf16[2,2,512,128]{3,2,1,0:T(8,128)(2,1)S(1)}, u32[]{:S(2)}, u32[]{:S(2)}) %collective-permute-start.2) | collective-permute-done | bytes 524320 | tf_op jit(solution)/shard_map/ppermute | solution.py:244
  28.7 0.1 shard_map.68
  28.8 4.3 %collective-permute-start.3 = (bf16[512,128]{1,0:T(8,128)(2,1)S(1)}, bf16[512,128]{1,0:T(8,128)(2,1)S(1)}, u32[]{:S(2)}, u32[]{:S(2)}) collective-permute-start(bf16[512,128]{1,0:T(8,128)(2,1)S(1)} %get-tuple-element.30), channel_id=1, source_target_pairs={{0,14},{2,12},{4,10},{6,8},{8,6},{10,4},{12,2},{14,0},{1,15},{3,13... | collective-permute-start | bytes 393224 | tf_op jit(solution)/shard_map/ppermute | solution.py:258
  33.0 0.0 collective-permute-start.4
  33.0 0.4 collective-permute-start.5
  33.4 13.0 %collective-permute-done.3.far_ref = bf16[512,128]{1,0:T(8,128)(2,1)S(1)} collective-permute-done((bf16[512,128]{1,0:T(8,128)(2,1)S(1)}, bf16[512,128]{1,0:T(8,128)(2,1)S(1)}, u32[]{:S(2)}, u32[]{:S(2)}) %collective-permute-start.3) | collective-permute-done | bytes 131104 | tf_op jit(solution)/shard_map/ppermute | solution.py:258
  46.4 2.2 %collective-permute-done.4.z_ref = bf16[512,128]{1,0:T(8,128)(2,1)S(1)} collective-permute-done((bf16[512,128]{1,0:T(8,128)(2,1)S(1)}, bf16[512,128]{1,0:T(8,128)(2,1)S(1)}, u32[]{:S(2)}, u32[]{:S(2)}) %collective-permute-start.4) | collective-permute-done | bytes 131104 | tf_op jit(solution)/shard_map/ppermute | solution.py:259
  48.6 0.0 collective-permute-done.5.both_ref
  48.6 0.0 all-to-all-done
  48.6 1.0 %shard_map.69 = bf16[128,512]{1,0:T(8,128)(2,1)} custom-call(f32[512,128]{1,0:T(8,128)S(1)} %get-tuple-element.29.mine_ref, bf16[512,128]{1,0:T(8,128)(2,1)S(1)} %collective-permute-done.3.far_ref, bf16[512,128]{1,0:T(8,128)(2,1)S(1)} %collective-permute-done.4.z_ref, bf16[512,128]{1,0:T(8,128)(2,1)S(1)} %collective-permute-done.5.both_ref, ...), custom_call_target="tpu_custom_call" | custom-call | flops 1048576 | bytes 4194304 | tf_op jit(solution)/shard_map/pallas_call | solution.py:170
Async XLA Ops:
  8.4 4.1 %collective-permute-start = (bf16[8,8,64,128]{3,2,1,0:T(8,128)(2,1)S(1)}, bf16[8,8,64,128]{3,2,1,0:T(8,128)(2,1)S(1)}, u32[]{:S(2)}, u32[]{:S(2)}) collective-permute-start(bf16[8,8,64,128]{3,2,1,0:T(8,128)(2,1)S(1)} %get-tuple-element.25), channel_id=1, source_target_pairs={{0,1},{1,0},{2,3},{3,2},{4,5},{5,4},{6,7},{7,6},{8,9},{9,8},{10,11... | collective-permute-start | bytes 3145736 | tf_op jit(solution)/shard_map/ppermute | solution.py:226
  12.5 2.9 %collective-permute-start.1 = (bf16[4,2,512,128]{3,2,1,0:T(8,128)(2,1)S(1)}, bf16[4,2,512,128]{3,2,1,0:T(8,128)(2,1)S(1)}, u32[]{:S(2)}, u32[]{:S(2)}) collective-permute-start(bf16[4,2,512,128]{3,2,1,0:T(8,128)(2,1)S(1)} %shard_map.65), channel_id=1, source_target_pairs={{0,1},{1,0},{2,3},{3,2},{4,5},{5,4},{6,7},{7,6},{8,9},{9,8},{10,11... | collective-permute-start | bytes 3145736 | tf_op jit(solution)/shard_map/ppermute | solution.py:229
  15.6 13.1 %collective-permute-start.2 = (bf16[2,2,512,128]{3,2,1,0:T(8,128)(2,1)S(1)}, bf16[2,2,512,128]{3,2,1,0:T(8,128)(2,1)S(1)}, u32[]{:S(2)}, u32[]{:S(2)}) collective-permute-start(bf16[2,2,512,128]{3,2,1,0:T(8,128)(2,1)S(1)} %get-tuple-element.28), channel_id=1, source_target_pairs={{0,4},{4,0},{8,12},{12,8},{1,5},{5,1},{9,13},{13,9},{2,6},{6,2},{1... | collective-permute-start | bytes 1572872 | tf_op jit(solution)/shard_map/ppermute | solution.py:244
  17.0 31.6 %all-to-all-start = ((bf16[64,64,128]{2,1,0:T(8,128)(2,1)}), bf16[64,64,128]{2,1,0:T(8,128)(2,1)S(1)}, u32[]{:S(2)}, u32[]{:S(2)}) async-start(bf16[64,64,128]{2,1,0:T(8,128)(2,1)} %bitcast.5), calls=%async_computation | async-start | bytes 2097152 | tf_op jit(solution)/shard_map/all_to_all | solution.py:246
  28.8 17.6 %collective-permute-start.3 = (bf16[512,128]{1,0:T(8,128)(2,1)S(1)}, bf16[512,128]{1,0:T(8,128)(2,1)S(1)}, u32[]{:S(2)}, u32[]{:S(2)}) collective-permute-start(bf16[512,128]{1,0:T(8,128)(2,1)S(1)} %get-tuple-element.30), channel_id=1, source_target_pairs={{0,14},{2,12},{4,10},{6,8},{8,6},{10,4},{12,2},{14,0},{1,15},{3,13... | collective-permute-start | bytes 393224 | tf_op jit(solution)/shard_map/ppermute | solution.py:258
  33.0 15.6 %collective-permute-start.4 = (bf16[512,128]{1,0:T(8,128)(2,1)S(1)}, bf16[512,128]{1,0:T(8,128)(2,1)S(1)}, u32[]{:S(2)}, u32[]{:S(2)}) collective-permute-start(bf16[512,128]{1,0:T(8,128)(2,1)S(1)} %get-tuple-element.31), channel_id=1, source_target_pairs={{0,12},{4,8},{8,4},{12,0},{1,13},{5,9},{9,5},{13,1},{2,14},{6,10},... | collective-permute-start | bytes 393224 | tf_op jit(solution)/shard_map/ppermute | solution.py:259
  33.0 15.6 %collective-permute-start.5 = (bf16[512,128]{1,0:T(8,128)(2,1)S(1)}, bf16[512,128]{1,0:T(8,128)(2,1)S(1)}, u32[]{:S(2)}, u32[]{:S(2)}) collective-permute-start(bf16[512,128]{1,0:T(8,128)(2,1)S(1)} %get-tuple-element.32), channel_id=1, source_target_pairs={{0,2},{2,0},{1,3},{3,1},{4,6},{6,4},{5,7},{7,5},{8,10},{10,8},{9,1... | collective-permute-start | bytes 393224 | tf_op jit(solution)/shard_map/ppermute | solution.py:260

commit v6 on v5

--- a/solution.py
+++ b/solution.py
@@ -99,7 +99,7 @@
     lax.fori_loop(0, slabs // 2, step, 0)
 
 
-def u_kernel(parity, tm_ref, p_ref, m_ref, out_ref):
+def u_kernel(parity, unroll, tm_ref, p_ref, m_ref, out_ref):
     y, zl = lax.axis_index("y"), lax.axis_index("zl")
     columns = pl.ds(pl.multiple_of(parity * LANES, LANES), LANES)
     near, far = y ^ 1, 3 - y
@@ -115,11 +115,11 @@
             out_ref[y_slot, z_slot] = u[:, i * LANES : (i + 1) * LANES].astype(out_ref.dtype)
         return carry
 
-    lax.fori_loop(0, p_ref.shape[0] // 4, step, 0)
+    lax.fori_loop(0, p_ref.shape[0] // 4, step, 0, unroll=unroll)
 
 
 def u_send_kernel(*refs):
-    u_kernel(1 - lax.axis_index("c"), *refs)
+    u_kernel(1 - lax.axis_index("c"), True, *refs)
 
 
 def u_keep_kernel(tm_ref, p_ref, m_ref, vk_ref, vg_ref, out_ref, v_hbm, v_ref, sem):
@@ -128,7 +128,7 @@
         v_ref[h] = (vk_ref[h] + vg_ref[h].astype(F32)).astype(BF16)
         copies.append(pltpu.make_async_copy(v_ref.at[h], v_hbm.at[h], sem.at[h]))
         copies[-1].start()
-    u_kernel(lax.axis_index("c"), tm_ref, p_ref, m_ref, out_ref)
+    u_kernel(lax.axis_index("c"), False, tm_ref, p_ref, m_ref, out_ref)
     for copy in copies:
         copy.wait()
 
@@ -146,7 +146,7 @@
         ref[...] = (rest_ref[slot, z] + more_ref[slot, z].astype(F32)).astype(ref.dtype)
 
 
-def last_kernel(mine_ref, far_ref, z_ref, both_ref, v_ref, out_ref, scratch):
+def v_sum_kernel(v_ref, out_ref, scratch):
     groups, slabs, block, _ = v_ref.shape
     own = block // groups
     for g in range(groups):
@@ -155,11 +155,15 @@
             v = v + v_ref[g, s].astype(F32)
         scratch[pl.ds(g * block, block), :] = v
     orbitals = groups * own
-    parts = [scratch[pl.ds(b, orbitals, stride=own), :] for b in range(own)]
-    u = mine_ref[...]
-    for ref in (far_ref, z_ref, both_ref):
-        u = u + ref[...].astype(F32)
-    out_ref[...] = (0.5 * (u + jnp.concatenate(parts, axis=0))).T.astype(BF16)
+    for b in range(own):
+        out_ref[pl.ds(b * orbitals, orbitals), :] = scratch[pl.ds(b, orbitals, stride=own), :]
+
+
+def last_kernel(mine_ref, both_ref, far_ref, z_ref, v_ref, out_ref):
+    total = mine_ref[...] + v_ref[...]
+    for ref in (both_ref, far_ref, z_ref):
+        total = total + ref[...].astype(F32)
+    out_ref[...] = (0.5 * total).T.astype(BF16)
 
 
 def held(x):
@@ -251,15 +255,17 @@
         [pltpu.VMEM(flat, F32)] + [jax.ShapeDtypeStruct(flat, BF16)] * 3,
         held(rest), u_more, flops=40 << 30,
     )
+    v_sum = call(
+        v_sum_kernel, pltpu.VMEM(flat, F32), v_all.reshape(v_shape), flops=4 << 30, scratch=[pltpu.VMEM(flat, F32)]
+    )
     return call(
         last_kernel,
         jax.ShapeDtypeStruct((LANES, rows), BF16),
-        mine,
+        held(mine),
         lax.ppermute(to_both, ("y", "zl"), far_z),
         lax.ppermute(to_far, "y", far),
         lax.ppermute(to_z, "zl", cores),
-        v_all.reshape(v_shape),
-        scratch=[pltpu.VMEM(flat, F32)],
+        held(v_sum),
     )
 
 

time: 49.8 us -> 49.4 us (level)
    ppermute x1, waiting for transfers between devices: 13 us -> 0.71 us  [body(): lax.ppermute(to_both, ('y', 'zl'), far_z)]
    all_to_all x1, waiting for transfers between devices: 0.01 us -> 12.1 us  [body(): lax.all_to_all(v_part.reshape(groups * slabs, block, LANES), ('x', 'zh',...]
    pallas_call x4 -> x5, Pallas kernels: 3.74 us -> 3.57 us  [call(): pl.pallas_call(kernel, in_specs=[VMEM] * len(operands), out_specs=jax.tre...]
  transfers between devices with their start and end apart: 7 -> 7, of which waited for: 3 -> 4; matrix products, arithmetic and copies ran while one was open for 0% -> 0% of each run, Pallas kernels for 11% -> 11%
where the time goes in v6:
time: 49.4 us; the launch traced here: 49.2 us
  starting transfers between devices  18.5 us (37%)
  waiting for transfers between devices  15.8 us (32%)
  Pallas kernels  14.8 us (30%)
    all_to_all x1, waiting for transfers between devices, body(): lax.all_to_all(v_part.reshape(groups * slabs, block, LANES), ('x', 'zh',...  12.1 us
    all_to_all x1, starting transfers between devices, body(): lax.all_to_all(v_part.reshape(groups * slabs, block, LANES), ('x', 'zh',...  10.8 us
    pallas_call x1, Pallas kernels, body(): pl.pallas_call(v_kernel, in_specs=[HBM] * 6, out_specs=[VMEM] * 5, out_sh...  8.43 us
    ppermute x1, starting transfers between devices, body(): lax.ppermute(to_both, ('y', 'zl'), far_z)  4.25 us
    pallas_call x5, Pallas kernels, call(): pl.pallas_call(kernel, in_specs=[VMEM] * len(operands), out_specs=jax.tre...  3.57 us
    pallas_call x1, Pallas kernels, body(): pl.pallas_call(u_keep_kernel, in_specs=[VMEM] * 5, out_specs=[VMEM, HBM],...  2.8 us
    ppermute x1, waiting for transfers between devices, body(): lax.ppermute(to_far, 'y', far)  2.21 us
    ppermute x1, starting transfers between devices, body(): v_got = lax.ppermute(v_send, 'c', cores)  1.49 us
  transfers between devices with their start and end apart: 7, of which 4 were waited for; matrix products, arithmetic and copies ran while one was open for 0% of the time, Pallas kernels for 11%

profile of v6, /device:TPU:1, one launch (start us, length us, event | category | flops | bytes accessed | tf_op | source)
XLA Modules:
  0.0 49.2 jit_solution(14858425753190703452)
XLA Ops:
  0.0 8.4 %shard_map.64 = (f32[8,8,64,128]{3,2,1,0:T(8,128)S(1)}, bf16[8,8,64,128]{3,2,1,0:T(8,128)(2,1)S(1)}, bf16[512,2048]{1,0:T(8,128)(2,1)S(1)}, bf16[8,2048,256]{2,1,0:T(8,128)(2,1)S(1)}, bf16[8,2048,256]{2,1,0:T(8,128)(2,1)S(1)}) custom-call(s32[1,64]{1,0:T(1,128)} %bitcast.7, s32[8,8]{1,0:T(8,128)} %map_hbm.1, s32[1,2048]{1,0:T(1,128)} %bitcast.6, ...), custom_call_target="tpu_custom_call" | custom-call | flops 4294967296 | bytes 20971520 | tf_op jit(solution)/shard_map/pallas_call | solution.py:197
  8.4 1.5 %collective-permute-start = (bf16[8,8,64,128]{3,2,1,0:T(8,128)(2,1)S(1)}, bf16[8,8,64,128]{3,2,1,0:T(8,128)(2,1)S(1)}, u32[]{:S(2)}, u32[]{:S(2)}) collective-permute-start(bf16[8,8,64,128]{3,2,1,0:T(8,128)(2,1)S(1)} %get-tuple-element.25), channel_id=1, source_target_pairs={{0,1},{1,0},{2,3},{3,2},{4,5},{5,4},{6,7},{7,6},{8,9},{9,8},{10,11... | collective-permute-start | bytes 3145736 | tf_op jit(solution)/shard_map/ppermute | solution.py:230
  9.9 2.4 %shard_map.65 = bf16[4,2,512,128]{3,2,1,0:T(8,128)(2,1)S(1)} custom-call(bf16[512,2048]{1,0:T(8,128)(2,1)S(1)} %get-tuple-element.20.refs_0_.tm_ref, bf16[8,2048,256]{2,1,0:T(8,128)(2,1)S(1)} %get-tuple-element.21.refs_1_.p_ref, bf16[8,2048,256]{2,1,0:T(8,128)(2,1)S(1)} %get-tuple-element.22.refs_2_.m_ref), custom_call_target="tpu_custom_call" | custom-call | flops 2147483648 | bytes 4194304 | tf_op jit(solution)/shard_map/pallas_call | solution.py:174
  12.3 0.1 collective-permute-start.1
  12.4 0.0 collective-permute-done.vg_ref
  12.4 2.8 %shard_map.66 = (f32[4,2,512,128]{3,2,1,0:T(8,128)S(1)}, bf16[8,8,64,128]{3,2,1,0:T(8,128)(2,1)}) custom-call(bf16[512,2048]{1,0:T(8,128)(2,1)S(1)} %get-tuple-element.20.refs_0_.tm_ref, bf16[8,2048,256]{2,1,0:T(8,128)(2,1)S(1)} %get-tuple-element.21.refs_1_.p_ref, bf16[8,2048,256]{2,1,0:T(8,128)(2,1)S(1)} %get-tuple-element.22.refs_2_.m_ref, ...), custom_call_target="tpu_custom_call" | custom-call | flops 2147483648 | bytes 4194304 | tf_op jit(solution)/shard_map/pallas_call | solution.py:234
  15.2 0.0 collective-permute-done.1.got_ref
  15.2 0.2 shard_map.67
  15.4 1.5 %collective-permute-start.2 = (bf16[2,2,512,128]{3,2,1,0:T(8,128)(2,1)S(1)}, bf16[2,2,512,128]{3,2,1,0:T(8,128)(2,1)S(1)}, u32[]{:S(2)}, u32[]{:S(2)}) collective-permute-start(bf16[2,2,512,128]{3,2,1,0:T(8,128)(2,1)S(1)} %get-tuple-element.28), channel_id=1, source_target_pairs={{0,4},{4,0},{8,12},{12,8},{1,5},{5,1},{9,13},{13,9},{2,6},{6,2},{1... | collective-permute-start | bytes 1572872 | tf_op jit(solution)/shard_map/ppermute | solution.py:248
  16.8 10.8 %all-to-all-start = ((bf16[64,64,128]{2,1,0:T(8,128)(2,1)}), bf16[64,64,128]{2,1,0:T(8,128)(2,1)S(1)}, u32[]{:S(2)}, u32[]{:S(2)}) async-start(bf16[64,64,128]{2,1,0:T(8,128)(2,1)} %bitcast.5), calls=%async_computation | async-start | bytes 2097152 | tf_op jit(solution)/shard_map/all_to_all | solution.py:250
  27.7 0.8 %collective-permute-done.2.more_ref = bf16[2,2,512,128]{3,2,1,0:T(8,128)(2,1)S(1)} collective-permute-done((bf16[2,2,512,128]{3,2,1,0:T(8,128)(2,1)S(1)}, bf16[2,2,512,128]{3,2,1,0:T(8,128)(2,1)S(1)}, u32[]{:S(2)}, u32[]{:S(2)}) %collective-permute-start.2) | collective-permute-done | bytes 524320 | tf_op jit(solution)/shard_map/ppermute | solution.py:248
  28.5 0.1 shard_map.68
  28.6 4.3 %collective-permute-start.3 = (bf16[512,128]{1,0:T(8,128)(2,1)S(1)}, bf16[512,128]{1,0:T(8,128)(2,1)S(1)}, u32[]{:S(2)}, u32[]{:S(2)}) collective-permute-start(bf16[512,128]{1,0:T(8,128)(2,1)S(1)} %get-tuple-element.30), channel_id=1, source_target_pairs={{0,14},{2,12},{4,10},{6,8},{8,6},{10,4},{12,2},{14,0},{1,15},{3,13... | collective-permute-start | bytes 393224 | tf_op jit(solution)/shard_map/ppermute | solution.py:265
  32.8 0.0 collective-permute-start.4
  32.8 0.4 collective-permute-start.5
  33.2 12.1 %all-to-all-done = bf16[64,64,128]{2,1,0:T(8,128)(2,1)S(1)} async-done(((bf16[64,64,128]{2,1,0:T(8,128)(2,1)}), bf16[64,64,128]{2,1,0:T(8,128)(2,1)S(1)}, u32[]{:S(2)}, u32[]{:S(2)}) %all-to-all-start) | async-done | bytes 1048608 | tf_op jit(solution)/shard_map/all_to_all | solution.py:250
  45.3 0.2 shard_map.69.v_ref
  45.5 0.7 %collective-permute-done.3.both_ref = bf16[512,128]{1,0:T(8,128)(2,1)S(1)} collective-permute-done((bf16[512,128]{1,0:T(8,128)(2,1)S(1)}, bf16[512,128]{1,0:T(8,128)(2,1)S(1)}, u32[]{:S(2)}, u32[]{:S(2)}) %collective-permute-start.3) | collective-permute-done | bytes 131104 | tf_op jit(solution)/shard_map/ppermute | solution.py:265
  46.2 2.2 %collective-permute-done.4.far_ref = bf16[512,128]{1,0:T(8,128)(2,1)S(1)} collective-permute-done((bf16[512,128]{1,0:T(8,128)(2,1)S(1)}, bf16[512,128]{1,0:T(8,128)(2,1)S(1)}, u32[]{:S(2)}, u32[]{:S(2)}) %collective-permute-start.4) | collective-permute-done | bytes 131104 | tf_op jit(solution)/shard_map/ppermute | solution.py:266
  48.4 0.0 collective-permute-done.5.z_ref
  48.4 0.8 %shard_map.70 = bf16[128,512]{1,0:T(8,128)(2,1)} custom-call(f32[512,128]{1,0:T(8,128)S(1)} %get-tuple-element.29.mine_ref, bf16[512,128]{1,0:T(8,128)(2,1)S(1)} %collective-permute-done.3.both_ref, bf16[512,128]{1,0:T(8,128)(2,1)S(1)} %collective-permute-done.4.far_ref, bf16[512,128]{1,0:T(8,128)(2,1)S(1)} %collective-permute-done.5.z_ref, ...), custom_call_target="tpu_custom_call" | custom-call | flops 1048576 | bytes 4194304 | tf_op jit(solution)/shard_map/pallas_call | solution.py:174
Async XLA Ops:
  8.4 4.0 %collective-permute-start = (bf16[8,8,64,128]{3,2,1,0:T(8,128)(2,1)S(1)}, bf16[8,8,64,128]{3,2,1,0:T(8,128)(2,1)S(1)}, u32[]{:S(2)}, u32[]{:S(2)}) collective-permute-start(bf16[8,8,64,128]{3,2,1,0:T(8,128)(2,1)S(1)} %get-tuple-element.25), channel_id=1, source_target_pairs={{0,1},{1,0},{2,3},{3,2},{4,5},{5,4},{6,7},{7,6},{8,9},{9,8},{10,11... | collective-permute-start | bytes 3145736 | tf_op jit(solution)/shard_map/ppermute | solution.py:230
  12.3 2.9 %collective-permute-start.1 = (bf16[4,2,512,128]{3,2,1,0:T(8,128)(2,1)S(1)}, bf16[4,2,512,128]{3,2,1,0:T(8,128)(2,1)S(1)}, u32[]{:S(2)}, u32[]{:S(2)}) collective-permute-start(bf16[4,2,512,128]{3,2,1,0:T(8,128)(2,1)S(1)} %shard_map.65), channel_id=1, source_target_pairs={{0,1},{1,0},{2,3},{3,2},{4,5},{5,4},{6,7},{7,6},{8,9},{9,8},{10,11... | collective-permute-start | bytes 3145736 | tf_op jit(solution)/shard_map/ppermute | solution.py:233
  15.4 13.1 %collective-permute-start.2 = (bf16[2,2,512,128]{3,2,1,0:T(8,128)(2,1)S(1)}, bf16[2,2,512,128]{3,2,1,0:T(8,128)(2,1)S(1)}, u32[]{:S(2)}, u32[]{:S(2)}) collective-permute-start(bf16[2,2,512,128]{3,2,1,0:T(8,128)(2,1)S(1)} %get-tuple-element.28), channel_id=1, source_target_pairs={{0,4},{4,0},{8,12},{12,8},{1,5},{5,1},{9,13},{13,9},{2,6},{6,2},{1... | collective-permute-start | bytes 1572872 | tf_op jit(solution)/shard_map/ppermute | solution.py:248
  16.8 28.5 %all-to-all-start = ((bf16[64,64,128]{2,1,0:T(8,128)(2,1)}), bf16[64,64,128]{2,1,0:T(8,128)(2,1)S(1)}, u32[]{:S(2)}, u32[]{:S(2)}) async-start(bf16[64,64,128]{2,1,0:T(8,128)(2,1)} %bitcast.5), calls=%async_computation | async-start | bytes 2097152 | tf_op jit(solution)/shard_map/all_to_all | solution.py:250
  28.6 17.6 %collective-permute-start.3 = (bf16[512,128]{1,0:T(8,128)(2,1)S(1)}, bf16[512,128]{1,0:T(8,128)(2,1)S(1)}, u32[]{:S(2)}, u32[]{:S(2)}) collective-permute-start(bf16[512,128]{1,0:T(8,128)(2,1)S(1)} %get-tuple-element.30), channel_id=1, source_target_pairs={{0,14},{2,12},{4,10},{6,8},{8,6},{10,4},{12,2},{14,0},{1,15},{3,13... | collective-permute-start | bytes 393224 | tf_op jit(solution)/shard_map/ppermute | solution.py:265
  32.8 15.6 %collective-permute-start.4 = (bf16[512,128]{1,0:T(8,128)(2,1)S(1)}, bf16[512,128]{1,0:T(8,128)(2,1)S(1)}, u32[]{:S(2)}, u32[]{:S(2)}) collective-permute-start(bf16[512,128]{1,0:T(8,128)(2,1)S(1)} %get-tuple-element.31), channel_id=1, source_target_pairs={{0,12},{4,8},{8,4},{12,0},{1,13},{5,9},{9,5},{13,1},{2,14},{6,10},... | collective-permute-start | bytes 393224 | tf_op jit(solution)/shard_map/ppermute | solution.py:266
  32.8 15.6 %collective-permute-start.5 = (bf16[512,128]{1,0:T(8,128)(2,1)S(1)}, bf16[512,128]{1,0:T(8,128)(2,1)S(1)}, u32[]{:S(2)}, u32[]{:S(2)}) collective-permute-start(bf16[512,128]{1,0:T(8,128)(2,1)S(1)} %get-tuple-element.32), channel_id=1, source_target_pairs={{0,2},{2,0},{1,3},{3,1},{4,6},{6,4},{5,7},{7,5},{8,10},{10,8},{9,1... | collective-permute-start | bytes 393224 | tf_op jit(solution)/shard_map/ppermute | solution.py:267

commit v7 on v6

--- a/solution.py
+++ b/solution.py
@@ -47,13 +47,21 @@
     return jnp.swapaxes(x.reshape(own, groups, own, LANES), 0, 1).reshape(shape)
 
 
-def v_kernel(
+def slot_of(s):
+    y, zl = lax.axis_index("y"), lax.axis_index("zl")
+    ys, zs = s // 2, s % 2
+    near, far = y ^ 1, 3 - y
+    y_slot = jnp.where(ys == y, 0, jnp.where(ys == far, 1, jnp.where(ys == near, 2, 3)))
+    return y_slot, jnp.where(zs == zl, 0, 1)
+
+
+def send_kernel(
     occ_hbm, map_hbm, col_hbm, t_hbm, p_hbm, m_hbm,
-    keep_ref, send_ref, tm_ref, p_ref, m_ref,
+    vs_ref, us_ref, tm_ref, p_ref, m_ref,
     occ_ref, map_ref, col_ref, label_ref, t_ref, small_sem, p_sem, m_sem,
 ):
     slabs = p_ref.shape[0]
-    groups, _, block, _ = keep_ref.shape
+    groups, _, block, _ = vs_ref.shape
     wide = 2 * LANES
     me = lax.axis_index("x") * lax.axis_size("zh") + lax.axis_index("zh")
     core = lax.axis_index("c")
@@ -82,53 +90,53 @@
     mask_rows(me, occ_ref, map_ref, col_ref, t_ref, tm_ref, label_ref)
     shape = (groups, block, LANES)
 
+    other = pl.ds(pl.multiple_of((1 - core) * LANES, LANES), LANES)
+
     def step(b, carry):
-        weights = []
+        less, more = [], []
         for i in range(2):
             for copy in loads(2 * b + i):
                 copy.wait()
-            weights.append(p_ref[2 * b + i] - m_ref[2 * b + i])
-        v = jnp.dot(tm_ref[...], jnp.concatenate(weights, axis=1), preferred_element_type=F32)
+            left, right = p_ref[2 * b + i, :, other], m_ref[2 * b + i, :, other]
+            less.append(left - right)
+            more.append(left + right)
+        both = jnp.dot(tm_ref[...], jnp.concatenate(less + more, axis=1), preferred_element_type=F32)
         for i in range(2):
-            low = v[:, 2 * i * LANES : (2 * i + 1) * LANES]
-            high = v[:, (2 * i + 1) * LANES : (2 * i + 2) * LANES]
-            keep_ref[:, 2 * b + i] = by_group(jnp.where(core == 0, low, high), shape)
-            send_ref[:, 2 * b + i] = by_group(jnp.where(core == 0, high, low), shape).astype(BF16)
+            vs_ref[:, 2 * b + i] = by_group(both[:, i * LANES : (i + 1) * LANES], shape).astype(BF16)
+            y_slot, z_slot = slot_of(2 * b + i)
+            us_ref[y_slot, z_slot] = both[:, (2 + i) * LANES : (3 + i) * LANES].astype(BF16)
         return carry
 
     lax.fori_loop(0, slabs // 2, step, 0)
 
 
-def u_kernel(parity, unroll, tm_ref, p_ref, m_ref, out_ref):
-    y, zl = lax.axis_index("y"), lax.axis_index("zl")
-    columns = pl.ds(pl.multiple_of(parity * LANES, LANES), LANES)
-    near, far = y ^ 1, 3 - y
+def u_kernel(tm_ref, p_ref, m_ref, out_ref):
+    columns = pl.ds(pl.multiple_of(lax.axis_index("c") * LANES, LANES), LANES)
 
     def step(b, carry):
         weights = [p_ref[4 * b + i, :, columns] + m_ref[4 * b + i, :, columns] for i in range(4)]
         u = jnp.dot(tm_ref[...], jnp.concatenate(weights, axis=1), preferred_element_type=F32)
         for i in range(4):
-            s = 4 * b + i
-            ys, zs = s // 2, s % 2
-            z_slot = jnp.where(zs == zl, 0, 1)
-            y_slot = jnp.where(ys == y, 0, jnp.where(ys == far, 1, jnp.where(ys == near, 2, 3)))
-            out_ref[y_slot, z_slot] = u[:, i * LANES : (i + 1) * LANES].astype(out_ref.dtype)
+            y_slot, z_slot = slot_of(4 * b + i)
+            out_ref[y_slot, z_slot] = u[:, i * LANES : (i + 1) * LANES]
         return carry
 
-    lax.fori_loop(0, p_ref.shape[0] // 4, step, 0, unroll=unroll)
-
-
-def u_send_kernel(*refs):
-    u_kernel(1 - lax.axis_index("c"), True, *refs)
-
-
-def u_keep_kernel(tm_ref, p_ref, m_ref, vk_ref, vg_ref, out_ref, v_hbm, v_ref, sem):
+    lax.fori_loop(0, p_ref.shape[0] // 4, step, 0, unroll=True)
+
+
+def v_kernel(tm_ref, p_ref, m_ref, got_ref, out_hbm, out_ref, sem):
+    groups, slabs, block, _ = out_ref.shape
+    columns = pl.ds(pl.multiple_of(lax.axis_index("c") * LANES, LANES), LANES)
     copies = []
-    for h in range(v_ref.shape[0]):
-        v_ref[h] = (vk_ref[h] + vg_ref[h].astype(F32)).astype(BF16)
-        copies.append(pltpu.make_async_copy(v_ref.at[h], v_hbm.at[h], sem.at[h]))
+    for b in range(slabs // 4):
+        weights = [p_ref[4 * b + i, :, columns] - m_ref[4 * b + i, :, columns] for i in range(4)]
+        v = jnp.dot(tm_ref[...], jnp.concatenate(weights, axis=1), preferred_element_type=F32)
+        for i in range(4):
+            own = by_group(v[:, i * LANES : (i + 1) * LANES], (groups, block, LANES))
+            out_ref[:, 4 * b + i] = (own + got_ref[:, 4 * b + i].astype(F32)).astype(BF16)
+        part = pl.ds(4 * b, 4)
+        copies.append(pltpu.make_async_copy(out_ref.at[:, part], out_hbm.at[:, part], sem.at[b]))
         copies[-1].start()
-    u_kernel(lax.axis_index("c"), False, tm_ref, p_ref, m_ref, out_ref)
     for copy in copies:
         copy.wait()
 
@@ -194,13 +202,13 @@
     v_shape, u_shape = (groups, slabs, block, LANES), (ys, zs, rows, LANES)
     wide = (slabs, depth, 2 * LANES)
     flops = rows * depth * width
-    v_keep, v_send, tm, p, m = pl.pallas_call(
-        v_kernel,
+    v_send, u_send, tm, p, m = pl.pallas_call(
+        send_kernel,
         in_specs=[HBM] * 6,
         out_specs=[VMEM] * 5,
         out_shape=[
-            pltpu.VMEM(v_shape, F32),
             pltpu.VMEM(v_shape, BF16),
+            pltpu.VMEM(u_shape, BF16),
             pltpu.VMEM((rows, depth), BF16),
             pltpu.VMEM(wide, BF16),
             pltpu.VMEM(wide, BF16),
@@ -227,26 +235,25 @@
     far = [(i, ys - 1 - i) for i in range(ys)]
     far_z = [(2 * a + z, 2 * b + 1 - z) for a, b in far for z in range(2)]
     flat = (rows, LANES)
+    factors = [held(x) for x in (p, m)]
+    u_got = lax.ppermute(u_send, "c", cores)
     v_got = lax.ppermute(v_send, "c", cores)
-    factors = [held(x) for x in (tm, p, m)]
-    u_send = call(u_send_kernel, pltpu.VMEM(u_shape, BF16), *factors, flops=flops)
-    u_got = lax.ppermute(u_send, "c", cores)
-    u_keep, v_part = pl.pallas_call(
-        u_keep_kernel,
-        in_specs=[VMEM] * 5,
-        out_specs=[VMEM, HBM],
-        out_shape=[pltpu.VMEM(u_shape, F32), pltpu.HBM(v_shape, BF16)],
-        scratch_shapes=[pltpu.VMEM(v_shape, BF16), pltpu.SemaphoreType.DMA((groups,))],
-        compiler_params=pltpu.CompilerParams(vmem_limit_bytes=8 * MIB),
-        cost_estimate=pl.CostEstimate(flops=flops, bytes_accessed=4 * MIB, transcendentals=0),
-    )(*factors, held(after(v_keep, u_send)), held(v_got))
+    u_keep = call(u_kernel, pltpu.VMEM(u_shape, F32), held(tm), *factors, flops=flops)
     u_out, rest = call(
         first_add_kernel,
         [jax.ShapeDtypeStruct((2, zs, *flat), BF16), pltpu.VMEM((2, zs, *flat), F32)],
         held(u_keep), held(u_got),
     )
     u_more = lax.ppermute(u_out, "y", near)
-    v_part = after(v_part, rest)
+    v_part = pl.pallas_call(
+        v_kernel,
+        in_specs=[VMEM] * 4,
+        out_specs=HBM,
+        out_shape=pltpu.HBM(v_shape, BF16),
+        scratch_shapes=[pltpu.VMEM(v_shape, BF16), pltpu.SemaphoreType.DMA((slabs // 4,))],
+        compiler_params=pltpu.CompilerParams(vmem_limit_bytes=8 * MIB),
+        cost_estimate=pl.CostEstimate(flops=flops, bytes_accessed=4 * MIB, transcendentals=0),
+    )(held(after(tm, rest)), *factors, held(v_got))
     v_all = lax.all_to_all(
         v_part.reshape(groups * slabs, block, LANES), ("x", "zh", "y", "zl"), 0, 0, tiled=True
     )

time: 49.4 us -> 49.3 us (level)
  starting transfers between devices: 18.5 us -> 17.9 us
  Pallas kernels: 14.8 us -> 15.4 us
    all_to_all x1, waiting for transfers between devices: 12.1 us -> 13.7 us  [body(): lax.all_to_all(v_part.reshape(groups * slabs, block, LANES), ('x', 'zh',...]
    ppermute x1, starting transfers between devices: 0.1 us -> 1.51 us  [body(): u_got = lax.ppermute(u_send, 'c', cores)]
    ppermute x1, starting transfers between devices: 1.49 us -> 0.09 us  [body(): v_got = lax.ppermute(v_send, 'c', cores)]
    ppermute x1, starting transfers between devices: 4.25 us -> 3.2 us  [body(): lax.ppermute(to_both, ('y', 'zl'), far_z)]
    ppermute x1, waiting for transfers between devices: 0.78 us -> 0.01 us  [body(): u_more = lax.ppermute(u_out, 'y', near)]
    ppermute x1, waiting for transfers between devices: 0.71 us -> 0.01 us  [body(): lax.ppermute(to_both, ('y', 'zl'), far_z)]
    pallas_call x2, Pallas kernels: 11.2 us -> 11.8 us  [the longest x1 8.6 us: body(): pl.pallas_call(send_kernel, in_specs=[HBM] * 6, out_specs=[VMEM] * 5, out...]
  transfers between devices with their start and end apart: 7 -> 7, of which waited for: 4 -> 3; matrix products, arithmetic and copies ran while one was open for 0% -> 0% of each run, Pallas kernels for 11% -> 12%
where the time goes in v7:
time: 49.3 us; the launch traced here: 49.1 us
  starting transfers between devices  17.9 us (36%)
  waiting for transfers between devices  15.7 us (32%)
  Pallas kernels  15.4 us (31%)
    all_to_all x1, waiting for transfers between devices, body(): lax.all_to_all(v_part.reshape(groups * slabs, block, LANES), ('x', 'zh',...  13.7 us
    all_to_all x1, starting transfers between devices, body(): lax.all_to_all(v_part.reshape(groups * slabs, block, LANES), ('x', 'zh',...  10.9 us
    pallas_call x1, Pallas kernels, body(): pl.pallas_call(send_kernel, in_specs=[HBM] * 6, out_specs=[VMEM] * 5, out...  8.6 us
    pallas_call x5, Pallas kernels, call(): pl.pallas_call(kernel, in_specs=[VMEM] * len(operands), out_specs=jax.tre...  3.57 us
    pallas_call x1, Pallas kernels, body(): pl.pallas_call(v_kernel, in_specs=[VMEM] * 4, out_specs=HBM, out_shape=pl...  3.22 us
    ppermute x1, starting transfers between devices, body(): lax.ppermute(to_both, ('y', 'zl'), far_z)  3.2 us
    ppermute x1, waiting for transfers between devices, body(): lax.ppermute(to_far, 'y', far)  1.86 us
    ppermute x1, starting transfers between devices, body(): u_got = lax.ppermute(u_send, 'c', cores)  1.51 us
  transfers between devices with their start and end apart: 7, of which 3 were waited for; matrix products, arithmetic and copies ran while one was open for 0% of the time, Pallas kernels for 12%

profile of v7, /device:TPU:1, one launch (start us, length us, event | category | flops | bytes accessed | tf_op | source)
XLA Modules:
  0.0 49.1 jit_solution(11917464182173228492)
XLA Ops:
  0.0 8.6 %shard_map.64 = (bf16[8,8,64,128]{3,2,1,0:T(8,128)(2,1)S(1)}, bf16[4,2,512,128]{3,2,1,0:T(8,128)(2,1)S(1)}, bf16[512,2048]{1,0:T(8,128)(2,1)S(1)}, bf16[8,2048,2...) custom-call(s32[1,64]{1,0:T(1,128)} %bitcast.7, s32[8,8]{1,0:T(8,128)} %map_hbm.1, s32[1,2048]{1,0:T(1,128)} %bitcast.6, ...), custom_call_target="tpu_custom_call" | custom-call | flops 4294967296 | bytes 20971520 | tf_op jit(solution)/shard_map/pallas_call | solution.py:205
  8.6 1.5 %collective-permute-start = (bf16[4,2,512,128]{3,2,1,0:T(8,128)(2,1)S(1)}, bf16[4,2,512,128]{3,2,1,0:T(8,128)(2,1)S(1)}, u32[]{:S(2)}, u32[]{:S(2)}) collective-permute-start(bf16[4,2,512,128]{3,2,1,0:T(8,128)(2,1)S(1)} %get-tuple-element.20), channel_id=1, source_target_pairs={{0,1},{1,0},{2,3},{3,2},{4,5},{5,4},{6,7},{7,6},{8,9},{9,8},{10,11... | collective-permute-start | bytes 3145736 | tf_op jit(solution)/shard_map/ppermute | solution.py:239
  10.1 0.1 collective-permute-start.5
  10.2 2.4 %shard_map.65.keep_ref = f32[4,2,512,128]{3,2,1,0:T(8,128)S(1)} custom-call(bf16[512,2048]{1,0:T(8,128)(2,1)S(1)} %get-tuple-element.27.tm_ref, bf16[8,2048,256]{2,1,0:T(8,128)(2,1)S(1)} %get-tuple-element.18.p_ref, bf16[8,2048,256]{2,1,0:T(8,128)(2,1)S(1)} %get-tuple-element.19.m_ref), custom_call_target="tpu_custom_call" | custom-call | flops 2147483648 | bytes 4194304 | tf_op jit(solution)/shard_map/pallas_call | solution.py:182
  12.6 0.0 collective-permute-done.got_ref
  12.6 0.2 shard_map.66
  12.8 1.5 %collective-permute-start.1 = (bf16[2,2,512,128]{3,2,1,0:T(8,128)(2,1)S(1)}, bf16[2,2,512,128]{3,2,1,0:T(8,128)(2,1)S(1)}, u32[]{:S(2)}, u32[]{:S(2)}) collective-permute-start(bf16[2,2,512,128]{3,2,1,0:T(8,128)(2,1)S(1)} %get-tuple-element.22), channel_id=1, source_target_pairs={{0,4},{4,0},{8,12},{12,8},{1,5},{5,1},{9,13},{13,9},{2,6},{6,2},{1... | collective-permute-start | bytes 1572872 | tf_op jit(solution)/shard_map/ppermute | solution.py:247
  14.2 0.0 collective-permute-done.5.got_ref
  14.2 3.2 %shard_map.68 = bf16[8,8,64,128]{3,2,1,0:T(8,128)(2,1)} custom-call(bf16[512,2048]{1,0:T(8,128)(2,1)S(1)} %get-tuple-element.27.tm_ref, bf16[8,2048,256]{2,1,0:T(8,128)(2,1)S(1)} %get-tuple-element.18.p_ref, bf16[8,2048,256]{2,1,0:T(8,128)(2,1)S(1)} %get-tuple-element.19.m_ref, bf16[8,8,64,128]{3,2,1,0:T(8,128)(2,1)S(1)} %collective-permute-done.5.got_ref), custom_call_target="tpu_custom_call" | custom-call | flops 2147483648 | bytes 4194304 | tf_op jit(solution)/shard_map/pallas_call | solution.py:248
  17.4 10.9 %all-to-all-start = ((bf16[64,64,128]{2,1,0:T(8,128)(2,1)}), bf16[64,64,128]{2,1,0:T(8,128)(2,1)S(1)}, u32[]{:S(2)}, u32[]{:S(2)}) async-start(bf16[64,64,128]{2,1,0:T(8,128)(2,1)} %bitcast.5), calls=%async_computation | async-start | bytes 2097152 | tf_op jit(solution)/shard_map/all_to_all | solution.py:257
  28.4 0.0 collective-permute-done.1.more_ref
  28.4 0.1 shard_map.67
  28.5 3.2 %collective-permute-start.2 = (bf16[512,128]{1,0:T(8,128)(2,1)S(1)}, bf16[512,128]{1,0:T(8,128)(2,1)S(1)}, u32[]{:S(2)}, u32[]{:S(2)}) collective-permute-start(bf16[512,128]{1,0:T(8,128)(2,1)S(1)} %get-tuple-element.24), channel_id=1, source_target_pairs={{0,14},{2,12},{4,10},{6,8},{8,6},{10,4},{12,2},{14,0},{1,15},{3,13... | collective-permute-start | bytes 393224 | tf_op jit(solution)/shard_map/ppermute | solution.py:272
  31.7 0.3 collective-permute-start.3
  31.9 0.5 collective-permute-start.4
  32.4 13.7 %all-to-all-done = bf16[64,64,128]{2,1,0:T(8,128)(2,1)S(1)} async-done(((bf16[64,64,128]{2,1,0:T(8,128)(2,1)}), bf16[64,64,128]{2,1,0:T(8,128)(2,1)S(1)}, u32[]{:S(2)}, u32[]{:S(2)}) %all-to-all-start) | async-done | bytes 1048608 | tf_op jit(solution)/shard_map/all_to_all | solution.py:257
  46.1 0.2 shard_map.69.v_ref
  46.2 0.0 collective-permute-done.2.both_ref
  46.2 1.9 %collective-permute-done.3.far_ref = bf16[512,128]{1,0:T(8,128)(2,1)S(1)} collective-permute-done((bf16[512,128]{1,0:T(8,128)(2,1)S(1)}, bf16[512,128]{1,0:T(8,128)(2,1)S(1)}, u32[]{:S(2)}, u32[]{:S(2)}) %collective-permute-start.3) | collective-permute-done | bytes 131104 | tf_op jit(solution)/shard_map/ppermute | solution.py:273
  48.1 0.1 collective-permute-done.4.z_ref
  48.2 0.8 %shard_map.70 = bf16[128,512]{1,0:T(8,128)(2,1)} custom-call(f32[512,128]{1,0:T(8,128)S(1)} %get-tuple-element.23.mine_ref, bf16[512,128]{1,0:T(8,128)(2,1)S(1)} %collective-permute-done.2.both_ref, bf16[512,128]{1,0:T(8,128)(2,1)S(1)} %collective-permute-done.3.far_ref, bf16[512,128]{1,0:T(8,128)(2,1)S(1)} %collective-permute-done.4.z_ref, ...), custom_call_target="tpu_custom_call" | custom-call | flops 1048576 | bytes 4194304 | tf_op jit(solution)/shard_map/pallas_call | solution.py:182
Async XLA Ops:
  8.6 4.0 %collective-permute-start = (bf16[4,2,512,128]{3,2,1,0:T(8,128)(2,1)S(1)}, bf16[4,2,512,128]{3,2,1,0:T(8,128)(2,1)S(1)}, u32[]{:S(2)}, u32[]{:S(2)}) collective-permute-start(bf16[4,2,512,128]{3,2,1,0:T(8,128)(2,1)S(1)} %get-tuple-element.20), channel_id=1, source_target_pairs={{0,1},{1,0},{2,3},{3,2},{4,5},{5,4},{6,7},{7,6},{8,9},{9,8},{10,11... | collective-permute-start | bytes 3145736 | tf_op jit(solution)/shard_map/ppermute | solution.py:239
  10.1 4.1 %collective-permute-start.5 = (bf16[8,8,64,128]{3,2,1,0:T(8,128)(2,1)S(1)}, bf16[8,8,64,128]{3,2,1,0:T(8,128)(2,1)S(1)}, u32[]{:S(2)}, u32[]{:S(2)}) collective-permute-start(bf16[8,8,64,128]{3,2,1,0:T(8,128)(2,1)S(1)} %get-tuple-element.28), channel_id=1, source_target_pairs={{0,1},{1,0},{2,3},{3,2},{4,5},{5,4},{6,7},{7,6},{8,9},{9,8},{10,11... | collective-permute-start | bytes 3145736 | tf_op jit(solution)/shard_map/ppermute | solution.py:240
  12.8 15.6 %collective-permute-start.1 = (bf16[2,2,512,128]{3,2,1,0:T(8,128)(2,1)S(1)}, bf16[2,2,512,128]{3,2,1,0:T(8,128)(2,1)S(1)}, u32[]{:S(2)}, u32[]{:S(2)}) collective-permute-start(bf16[2,2,512,128]{3,2,1,0:T(8,128)(2,1)S(1)} %get-tuple-element.22), channel_id=1, source_target_pairs={{0,4},{4,0},{8,12},{12,8},{1,5},{5,1},{9,13},{13,9},{2,6},{6,2},{1... | collective-permute-start | bytes 1572872 | tf_op jit(solution)/shard_map/ppermute | solution.py:247
  17.4 28.6 %all-to-all-start = ((bf16[64,64,128]{2,1,0:T(8,128)(2,1)}), bf16[64,64,128]{2,1,0:T(8,128)(2,1)S(1)}, u32[]{:S(2)}, u32[]{:S(2)}) async-start(bf16[64,64,128]{2,1,0:T(8,128)(2,1)} %bitcast.5), calls=%async_computation | async-start | bytes 2097152 | tf_op jit(solution)/shard_map/all_to_all | solution.py:257
  28.5 17.8 %collective-permute-start.2 = (bf16[512,128]{1,0:T(8,128)(2,1)S(1)}, bf16[512,128]{1,0:T(8,128)(2,1)S(1)}, u32[]{:S(2)}, u32[]{:S(2)}) collective-permute-start(bf16[512,128]{1,0:T(8,128)(2,1)S(1)} %get-tuple-element.24), channel_id=1, source_target_pairs={{0,14},{2,12},{4,10},{6,8},{8,6},{10,4},{12,2},{14,0},{1,15},{3,13... | collective-permute-start | bytes 393224 | tf_op jit(solution)/shard_map/ppermute | solution.py:272
  31.7 16.4 %collective-permute-start.3 = (bf16[512,128]{1,0:T(8,128)(2,1)S(1)}, bf16[512,128]{1,0:T(8,128)(2,1)S(1)}, u32[]{:S(2)}, u32[]{:S(2)}) collective-permute-start(bf16[512,128]{1,0:T(8,128)(2,1)S(1)} %get-tuple-element.25), channel_id=1, source_target_pairs={{0,12},{4,8},{8,4},{12,0},{1,13},{5,9},{9,5},{13,1},{2,14},{6,10},... | collective-permute-start | bytes 393224 | tf_op jit(solution)/shard_map/ppermute | solution.py:273
  31.9 16.3 %collective-permute-start.4 = (bf16[512,128]{1,0:T(8,128)(2,1)S(1)}, bf16[512,128]{1,0:T(8,128)(2,1)S(1)}, u32[]{:S(2)}, u32[]{:S(2)}) collective-permute-start(bf16[512,128]{1,0:T(8,128)(2,1)S(1)} %get-tuple-element.26), channel_id=1, source_target_pairs={{0,2},{2,0},{1,3},{3,1},{4,6},{6,4},{5,7},{7,5},{8,10},{10,8},{9,1... | collective-permute-start | bytes 393224 | tf_op jit(solution)/shard_map/ppermute | solution.py:274

commit v8 on v7

--- a/solution.py
+++ b/solution.py
@@ -167,11 +167,19 @@
         out_ref[pl.ds(b * orbitals, orbitals), :] = scratch[pl.ds(b, orbitals, stride=own), :]
 
 
-def last_kernel(mine_ref, both_ref, far_ref, z_ref, v_ref, out_ref):
-    total = mine_ref[...] + v_ref[...]
-    for ref in (both_ref, far_ref, z_ref):
-        total = total + ref[...].astype(F32)
-    out_ref[...] = (0.5 * total).T.astype(BF16)
+def last_kernel(mine_ref, both_ref, far_ref, z_ref, v_ref, out_hbm, out_ref, sem):
+    half = mine_ref.shape[0] // 2
+    copies = []
+    for i in range(2):
+        rows = pl.ds(i * half, half)
+        total = mine_ref[rows, :] + v_ref[rows, :]
+        for ref in (both_ref, far_ref, z_ref):
+            total = total + ref[rows, :].astype(F32)
+        out_ref[i] = (0.5 * total).T.astype(BF16)
+        copies.append(pltpu.make_async_copy(out_ref.at[i], out_hbm.at[:, rows], sem.at[i]))
+        copies[-1].start()
+    for copy in copies:
+        copy.wait()
 
 
 def held(x):
@@ -265,9 +273,14 @@
     v_sum = call(
         v_sum_kernel, pltpu.VMEM(flat, F32), v_all.reshape(v_shape), flops=4 << 30, scratch=[pltpu.VMEM(flat, F32)]
     )
-    return call(
+    return pl.pallas_call(
         last_kernel,
-        jax.ShapeDtypeStruct((LANES, rows), BF16),
+        in_specs=[VMEM] * 5,
+        out_specs=HBM,
+        out_shape=jax.ShapeDtypeStruct((LANES, rows), BF16),
+        scratch_shapes=[pltpu.VMEM((2, LANES, rows // 2), BF16), pltpu.SemaphoreType.DMA((2,))],
+        compiler_params=pltpu.CompilerParams(vmem_limit_bytes=8 * MIB),
+    )(
         held(mine),
         lax.ppermute(to_both, ("y", "zl"), far_z),
         lax.ppermute(to_far, "y", far),

time: 49.3 us -> 49.3 us (level)
    pallas_call x0 -> x1, Pallas kernels: none -> 0.81 us  [body(): pl.pallas_call(last_kernel, in_specs=[VMEM] * 5, out_specs=HBM, out_shape...]
    pallas_call x5 -> x4, Pallas kernels: 3.57 us -> 2.77 us  [call(): pl.pallas_call(kernel, in_specs=[VMEM] * len(operands), out_specs=jax.tre...]
where the time goes in v8:
time: 49.3 us; the launch traced here: 49.1 us
  starting transfers between devices  17.9 us (36%)
  waiting for transfers between devices  15.7 us (32%)
  Pallas kernels  15.4 us (31%)
    all_to_all x1, waiting for transfers between devices, body(): lax.all_to_all(v_part.reshape(groups * slabs, block, LANES), ('x', 'zh',...  13.7 us
    all_to_all x1, starting transfers between devices, body(): lax.all_to_all(v_part.reshape(groups * slabs, block, LANES), ('x', 'zh',...  10.9 us
    pallas_call x1, Pallas kernels, body(): pl.pallas_call(send_kernel, in_specs=[HBM] * 6, out_specs=[VMEM] * 5, out...  8.6 us
    pallas_call x1, Pallas kernels, body(): pl.pallas_call(v_kernel, in_specs=[VMEM] * 4, out_specs=HBM, out_shape=pl...  3.22 us
    ppermute x1, starting transfers between devices, body(): lax.ppermute(to_both, ('y', 'zl'), far_z)  3.2 us
    pallas_call x4, Pallas kernels, call(): pl.pallas_call(kernel, in_specs=[VMEM] * len(operands), out_specs=jax.tre...  2.77 us
    ppermute x1, waiting for transfers between devices, body(): lax.ppermute(to_far, 'y', far)  1.86 us
    ppermute x1, starting transfers between devices, body(): u_got = lax.ppermute(u_send, 'c', cores)  1.51 us
  transfers between devices with their start and end apart: 7, of which 3 were waited for; matrix products, arithmetic and copies ran while one was open for 0% of the time, Pallas kernels for 12%

profile of v8, /device:TPU:1, one launch (start us, length us, event | category | flops | bytes accessed | tf_op | source)
XLA Modules:
  0.0 49.1 jit_solution(15305324616765211404)
XLA Ops:
  0.0 8.6 %shard_map.64 = (bf16[8,8,64,128]{3,2,1,0:T(8,128)(2,1)S(1)}, bf16[4,2,512,128]{3,2,1,0:T(8,128)(2,1)S(1)}, bf16[512,2048]{1,0:T(8,128)(2,1)S(1)}, bf16[8,2048,2...) custom-call(s32[1,64]{1,0:T(1,128)} %bitcast.7, s32[8,8]{1,0:T(8,128)} %map_hbm.1, s32[1,2048]{1,0:T(1,128)} %bitcast.6, ...), custom_call_target="tpu_custom_call" | custom-call | flops 4294967296 | bytes 20971520 | tf_op jit(solution)/shard_map/pallas_call | solution.py:213
  8.6 1.5 %collective-permute-start = (bf16[4,2,512,128]{3,2,1,0:T(8,128)(2,1)S(1)}, bf16[4,2,512,128]{3,2,1,0:T(8,128)(2,1)S(1)}, u32[]{:S(2)}, u32[]{:S(2)}) collective-permute-start(bf16[4,2,512,128]{3,2,1,0:T(8,128)(2,1)S(1)} %get-tuple-element.20), channel_id=1, source_target_pairs={{0,1},{1,0},{2,3},{3,2},{4,5},{5,4},{6,7},{7,6},{8,9},{9,8},{10,11... | collective-permute-start | bytes 3145736 | tf_op jit(solution)/shard_map/ppermute | solution.py:247
  10.1 0.1 collective-permute-start.5
  10.2 2.4 %shard_map.65.keep_ref = f32[4,2,512,128]{3,2,1,0:T(8,128)S(1)} custom-call(bf16[512,2048]{1,0:T(8,128)(2,1)S(1)} %get-tuple-element.27.tm_ref, bf16[8,2048,256]{2,1,0:T(8,128)(2,1)S(1)} %get-tuple-element.18.p_ref, bf16[8,2048,256]{2,1,0:T(8,128)(2,1)S(1)} %get-tuple-element.19.m_ref), custom_call_target="tpu_custom_call" | custom-call | flops 2147483648 | bytes 4194304 | tf_op jit(solution)/shard_map/pallas_call | solution.py:190
  12.6 0.0 collective-permute-done.got_ref
  12.6 0.2 shard_map.66
  12.8 1.5 %collective-permute-start.1 = (bf16[2,2,512,128]{3,2,1,0:T(8,128)(2,1)S(1)}, bf16[2,2,512,128]{3,2,1,0:T(8,128)(2,1)S(1)}, u32[]{:S(2)}, u32[]{:S(2)}) collective-permute-start(bf16[2,2,512,128]{3,2,1,0:T(8,128)(2,1)S(1)} %get-tuple-element.22), channel_id=1, source_target_pairs={{0,4},{4,0},{8,12},{12,8},{1,5},{5,1},{9,13},{13,9},{2,6},{6,2},{1... | collective-permute-start | bytes 1572872 | tf_op jit(solution)/shard_map/ppermute | solution.py:255
  14.2 0.0 collective-permute-done.5.got_ref
  14.2 3.2 %shard_map.68 = bf16[8,8,64,128]{3,2,1,0:T(8,128)(2,1)} custom-call(bf16[512,2048]{1,0:T(8,128)(2,1)S(1)} %get-tuple-element.27.tm_ref, bf16[8,2048,256]{2,1,0:T(8,128)(2,1)S(1)} %get-tuple-element.18.p_ref, bf16[8,2048,256]{2,1,0:T(8,128)(2,1)S(1)} %get-tuple-element.19.m_ref, bf16[8,8,64,128]{3,2,1,0:T(8,128)(2,1)S(1)} %collective-permute-done.5.got_ref), custom_call_target="tpu_custom_call" | custom-call | flops 2147483648 | bytes 4194304 | tf_op jit(solution)/shard_map/pallas_call | solution.py:256
  17.4 10.9 %all-to-all-start = ((bf16[64,64,128]{2,1,0:T(8,128)(2,1)}), bf16[64,64,128]{2,1,0:T(8,128)(2,1)S(1)}, u32[]{:S(2)}, u32[]{:S(2)}) async-start(bf16[64,64,128]{2,1,0:T(8,128)(2,1)} %bitcast.5), calls=%async_computation | async-start | bytes 2097152 | tf_op jit(solution)/shard_map/all_to_all | solution.py:265
  28.4 0.0 collective-permute-done.1.more_ref
  28.4 0.1 shard_map.67
  28.5 3.2 %collective-permute-start.2 = (bf16[512,128]{1,0:T(8,128)(2,1)S(1)}, bf16[512,128]{1,0:T(8,128)(2,1)S(1)}, u32[]{:S(2)}, u32[]{:S(2)}) collective-permute-start(bf16[512,128]{1,0:T(8,128)(2,1)S(1)} %get-tuple-element.24), channel_id=1, source_target_pairs={{0,14},{2,12},{4,10},{6,8},{8,6},{10,4},{12,2},{14,0},{1,15},{3,13... | collective-permute-start | bytes 393224 | tf_op jit(solution)/shard_map/ppermute | solution.py:285
  31.7 0.3 collective-permute-start.3
  31.9 0.5 collective-permute-start.4
  32.4 13.7 %all-to-all-done = bf16[64,64,128]{2,1,0:T(8,128)(2,1)S(1)} async-done(((bf16[64,64,128]{2,1,0:T(8,128)(2,1)}), bf16[64,64,128]{2,1,0:T(8,128)(2,1)S(1)}, u32[]{:S(2)}, u32[]{:S(2)}) %all-to-all-start) | async-done | bytes 1048608 | tf_op jit(solution)/shard_map/all_to_all | solution.py:265
  46.1 0.2 shard_map.69.v_ref
  46.2 0.0 collective-permute-done.2.both_ref
  46.2 1.9 %collective-permute-done.3.far_ref = bf16[512,128]{1,0:T(8,128)(2,1)S(1)} collective-permute-done((bf16[512,128]{1,0:T(8,128)(2,1)S(1)}, bf16[512,128]{1,0:T(8,128)(2,1)S(1)}, u32[]{:S(2)}, u32[]{:S(2)}) %collective-permute-start.3) | collective-permute-done | bytes 131104 | tf_op jit(solution)/shard_map/ppermute | solution.py:286
  48.1 0.1 collective-permute-done.4.z_ref
  48.2 0.8 %shard_map.70 = bf16[128,512]{1,0:T(8,128)(2,1)} custom-call(f32[512,128]{1,0:T(8,128)S(1)} %get-tuple-element.23.mine_ref, bf16[512,128]{1,0:T(8,128)(2,1)S(1)} %collective-permute-done.2.both_ref, bf16[512,128]{1,0:T(8,128)(2,1)S(1)} %collective-permute-done.3.far_ref, bf16[512,128]{1,0:T(8,128)(2,1)S(1)} %collective-permute-done.4.z_ref, ...), custom_call_target="tpu_custom_call" | custom-call | tf_op jit(solution)/shard_map/pallas_call | solution.py:276
Async XLA Ops:
  8.6 4.0 %collective-permute-start = (bf16[4,2,512,128]{3,2,1,0:T(8,128)(2,1)S(1)}, bf16[4,2,512,128]{3,2,1,0:T(8,128)(2,1)S(1)}, u32[]{:S(2)}, u32[]{:S(2)}) collective-permute-start(bf16[4,2,512,128]{3,2,1,0:T(8,128)(2,1)S(1)} %get-tuple-element.20), channel_id=1, source_target_pairs={{0,1},{1,0},{2,3},{3,2},{4,5},{5,4},{6,7},{7,6},{8,9},{9,8},{10,11... | collective-permute-start | bytes 3145736 | tf_op jit(solution)/shard_map/ppermute | solution.py:247
  10.1 4.1 %collective-permute-start.5 = (bf16[8,8,64,128]{3,2,1,0:T(8,128)(2,1)S(1)}, bf16[8,8,64,128]{3,2,1,0:T(8,128)(2,1)S(1)}, u32[]{:S(2)}, u32[]{:S(2)}) collective-permute-start(bf16[8,8,64,128]{3,2,1,0:T(8,128)(2,1)S(1)} %get-tuple-element.28), channel_id=1, source_target_pairs={{0,1},{1,0},{2,3},{3,2},{4,5},{5,4},{6,7},{7,6},{8,9},{9,8},{10,11... | collective-permute-start | bytes 3145736 | tf_op jit(solution)/shard_map/ppermute | solution.py:248
  12.8 15.6 %collective-permute-start.1 = (bf16[2,2,512,128]{3,2,1,0:T(8,128)(2,1)S(1)}, bf16[2,2,512,128]{3,2,1,0:T(8,128)(2,1)S(1)}, u32[]{:S(2)}, u32[]{:S(2)}) collective-permute-start(bf16[2,2,512,128]{3,2,1,0:T(8,128)(2,1)S(1)} %get-tuple-element.22), channel_id=1, source_target_pairs={{0,4},{4,0},{8,12},{12,8},{1,5},{5,1},{9,13},{13,9},{2,6},{6,2},{1... | collective-permute-start | bytes 1572872 | tf_op jit(solution)/shard_map/ppermute | solution.py:255
  17.4 28.6 %all-to-all-start = ((bf16[64,64,128]{2,1,0:T(8,128)(2,1)}), bf16[64,64,128]{2,1,0:T(8,128)(2,1)S(1)}, u32[]{:S(2)}, u32[]{:S(2)}) async-start(bf16[64,64,128]{2,1,0:T(8,128)(2,1)} %bitcast.5), calls=%async_computation | async-start | bytes 2097152 | tf_op jit(solution)/shard_map/all_to_all | solution.py:265
  28.5 17.8 %collective-permute-start.2 = (bf16[512,128]{1,0:T(8,128)(2,1)S(1)}, bf16[512,128]{1,0:T(8,128)(2,1)S(1)}, u32[]{:S(2)}, u32[]{:S(2)}) collective-permute-start(bf16[512,128]{1,0:T(8,128)(2,1)S(1)} %get-tuple-element.24), channel_id=1, source_target_pairs={{0,14},{2,12},{4,10},{6,8},{8,6},{10,4},{12,2},{14,0},{1,15},{3,13... | collective-permute-start | bytes 393224 | tf_op jit(solution)/shard_map/ppermute | solution.py:285
  31.7 16.4 %collective-permute-start.3 = (bf16[512,128]{1,0:T(8,128)(2,1)S(1)}, bf16[512,128]{1,0:T(8,128)(2,1)S(1)}, u32[]{:S(2)}, u32[]{:S(2)}) collective-permute-start(bf16[512,128]{1,0:T(8,128)(2,1)S(1)} %get-tuple-element.25), channel_id=1, source_target_pairs={{0,12},{4,8},{8,4},{12,0},{1,13},{5,9},{9,5},{13,1},{2,14},{6,10},... | collective-permute-start | bytes 393224 | tf_op jit(solution)/shard_map/ppermute | solution.py:286
  31.9 16.3 %collective-permute-start.4 = (bf16[512,128]{1,0:T(8,128)(2,1)S(1)}, bf16[512,128]{1,0:T(8,128)(2,1)S(1)}, u32[]{:S(2)}, u32[]{:S(2)}) collective-permute-start(bf16[512,128]{1,0:T(8,128)(2,1)S(1)} %get-tuple-element.26), channel_id=1, source_target_pairs={{0,2},{2,0},{1,3},{3,1},{4,6},{6,4},{5,7},{7,5},{8,10},{10,8},{9,1... | collective-permute-start | bytes 393224 | tf_op jit(solution)/shard_map/ppermute | solution.py:287
